TPU v7x, 32 devices: a whole 2x2x4 slice. The times are simulated.
32 devices in a mesh: row: 4 (over x, core), col: 8 (over z, y).
Axes of the slice: x: 2, y: 2, z: 4, core: 2. Of those that a mesh axis runs over, the one named last changes fastest.
Arguments:
- right_side: float32 [32768, 128], P(('row', 'col')), may hold values from -6 to 6
- leaf_inverse: bfloat16 [32768, 1024], P(('row', 'col')), may hold values from -0.1875 to 0.1875
- compress: bfloat16 [32768, 1024], P(('row', 'col')), may hold values from -0.1875 to 0.1875
- middle: bfloat16 [32768, 1024], P(('row', 'col')), may hold values from -0.1875 to 0.1875
- expand: bfloat16 [32768, 1024], P(('row', 'col')), may hold values from -0.1875 to 0.1875
- row_project: bfloat16 [2, 32768, 256], P(None, ('row', 'col')), may hold values from -0.1875 to 0.1875
- row_expand: bfloat16 [2, 32768, 256], P(None, ('row', 'col')), may hold values from -0.25 to 0.25
- root_project: bfloat16 [32768, 256], P(('row', 'col')), may hold values from -0.03125 to 0.03125
- root_expand: bfloat16 [32768, 256], P(('row', 'col')), may hold values from -0.375 to 0.375
- owner_map: int32 [8], replicated, may hold values from 0 to 7, each once
Outputs:
- applied: float32 [32768, 128], P(('row', 'col'))
Inputs may be any that keep to these rules, and one draw needn't show every extreme that they name: owner_map names each of the 8 column positions exactly once.
All inputs are finite; a program needn't handle non-finite values.
Results may differ from a plain program's by a relative error of at most 0.004.
Values may be sent and summed in bfloat16 or wider, within the bound.
No kernel may reach another device: no remote copies, remote signals or barrier semaphores. Data moves between devices by JAX's collectives and lax.ppermute only.
A program may use at most 128 MiB of HBM per device.

v0:
```python
import jax
import jax.numpy as jnp
from jax import lax
from jax.sharding import PartitionSpec as P

contract_first = (((0,), (0,)), ((), ()))


def swapped(x, axis, bit):
    return lax.ppermute(x, axis, [(i, i ^ 1 << bit) for i in range(lax.axis_size(axis))])


def per_device(
    right_side,
    leaf_inverse,
    compress,
    middle,
    expand,
    row_project,
    row_expand,
    root_project,
    root_expand,
    owner_map,
):
    lowered = right_side.astype(jnp.bfloat16)
    columns = lowered.shape[1]
    dense_part = jnp.dot(leaf_inverse, lowered, preferred_element_type=jnp.float32)
    coeffs = lax.dot_general(
        compress, lowered, contract_first, preferred_element_type=jnp.float32
    ).astype(jnp.bfloat16)
    col_count = lax.axis_size("col")
    pieces = coeffs.reshape(col_count, -1, columns)
    inverse = jnp.argsort(owner_map)
    outgoing = jnp.take(pieces, inverse, axis=0)
    arrived = lax.all_to_all(outgoing, "col", split_axis=0, concat_axis=0, tiled=True)
    shape_now = arrived.shape
    mixed_rows = jnp.dot(
        middle, arrived.reshape(-1, shape_now[2]), preferred_element_type=jnp.float32
    )
    mixed_rows = mixed_rows.astype(jnp.bfloat16).reshape(shape_now)
    returned = lax.all_to_all(mixed_rows, "col", split_axis=0, concat_axis=0, tiled=True)
    ordered = jnp.take(returned, owner_map, axis=0).reshape(-1, columns)
    cluster_part = jnp.dot(expand, ordered, preferred_element_type=jnp.float32)
    level_coeffs = jnp.einsum(
        "blr,lw->brw", row_project, lowered, preferred_element_type=jnp.float32
    )
    root_term = lax.dot_general(
        root_project, lowered, contract_first, preferred_element_type=jnp.float32
    )
    levels = lax.axis_size("row").bit_length() - 1
    running = level_coeffs
    siblings = []
    for level_bit in range(levels):
        partner = swapped(running[level_bit:], "row", level_bit)
        siblings.append(partner[0])
        running = jnp.concatenate(
            [running[: level_bit + 1], running[level_bit + 1 :] + partner[1:]], axis=0
        )
    sibling_sum = jnp.stack(siblings, axis=0)
    root_sum = lax.psum(root_term, ("row", "col"))
    coupled = jnp.einsum(
        "blr,brw->lw",
        row_expand,
        sibling_sum.astype(jnp.bfloat16),
        preferred_element_type=jnp.float32,
    )
    root_part = jnp.dot(
        root_expand, root_sum.astype(jnp.bfloat16), preferred_element_type=jnp.float32
    )
    return dense_part + cluster_part + coupled + root_part


def solution(mesh):
    in_specs = (
        P(("row", "col"), None),
        P(("row", "col"), None),
        P(("row", "col"), None),
        P(("row", "col"), None),
        P(("row", "col"), None),
        P(None, ("row", "col"), None),
        P(None, ("row", "col"), None),
        P(("row", "col"), None),
        P(("row", "col"), None),
        P(),
    )
    out_specs = P(("row", "col"), None)
    return jax.shard_map(
        per_device, mesh=mesh, in_specs=in_specs, out_specs=out_specs, check_vma=False
    )
```

profile of v0, /device:TPU:0, one launch (start us, length us, event | category | flops | bytes accessed | tf_op | source)
XLA Modules:
  0.0 81.0 jit_solution(1463292162804927002)
XLA Ops:
  0.0 0.0 copy-start
  0.0 0.0 copy-start.4
  0.0 1.2 %convert_element_type.16 = bf16[1024,128]{1,0:T(8,128)(2,1)S(1)} convert(f32[1024,128]{1,0:T(8,128)} %param.12) | non-fusion elementwise | flops 131072 | bytes 786432 | tf_op jit(solution)/shard_map/convert_element_type | solution.py:25
  1.2 1.7 %fusion.4 = f32[2,256,128]{2,1,0:T(8,128)S(1)} fusion(bf16[2,1024,256]{2,1,0:T(8,128)(2,1)} %param.17, bf16[1024,128]{1,0:T(8,128)(2,1)S(1)} %convert_element_type.16), kind=kOutput, calls=%fused_computation.11 | convolution fusion | flops 134217728 | bytes 1572864 | tf_op jit(solution)/shard_map/blr,lw->brw/dot_general | solution.py:44
  2.9 0.5 collective-permute-start
  3.5 0.0 copy-done.4
  3.5 1.0 %sort.17 = (s32[8]{0:T(128)}, s32[8]{0:T(128)S(1)}) sort(s32[8]{0:T(128)S(1)} %copy-done.4, s32[8]{0:T(128)S(1)} %iota.4), dimensions={0}, to_apply=%region_0.0 | sort | flops 24 | bytes 128 | tf_op jit(solution)/shard_map/jit(argsort)/sort | solution.py:33
  4.4 0.0 copy-done
  4.4 0.8 convolution_convert_fusion.1
  5.2 0.6 gather_fusion
  5.8 0.8 broadcast_select_fusion.1
  6.6 6.9 %all-to-all-start = ((bf16[8,128,128]{2,1,0:T(8,128)(2,1)}), bf16[8,128,128]{2,1,0:T(8,128)(2,1)S(1)}, u32[]{:S(2)}, u32[]{:S(2)}) async-start(bf16[8,128,128]{2,1,0:T(8,128)(2,1)} %broadcast_select_fusion.1), calls=%async_computation | async-start | bytes 524288 | tf_op jit(solution)/shard_map/all_to_all | solution.py:35
  13.5 1.4 %fusion.13 = f32[256,128]{1,0:T(8,128)S(1)} fusion(bf16[1024,256]{1,0:T(8,128)(2,1)} %param.19, bf16[1024,128]{1,0:T(8,128)(2,1)S(1)} %convert_element_type.16), kind=kOutput, calls=%fused_computation.30 | convolution fusion | flops 67108864 | bytes 917504 | tf_op jit(solution)/shard_map/dot_general | solution.py:47
  14.9 2.3 %fusion.12 = f32[1024,128]{1,0:T(8,128)S(1)} fusion(bf16[1024,1024]{1,0:T(8,128)(2,1)} %param.13, bf16[1024,128]{1,0:T(8,128)(2,1)S(1)} %convert_element_type.16), kind=kOutput, calls=%fused_computation.29 | convolution fusion | flops 268435456 | bytes 2883584 | tf_op jit(solution)/shard_map/dot_general | solution.py:27
  17.2 5.9 %all-to-all-done = bf16[8,128,128]{2,1,0:T(8,128)(2,1)S(1)} async-done(((bf16[8,128,128]{2,1,0:T(8,128)(2,1)}), bf16[8,128,128]{2,1,0:T(8,128)(2,1)S(1)}, u32[]{:S(2)}, u32[]{:S(2)}) %all-to-all-start) | async-done | bytes 262176 | tf_op jit(solution)/shard_map/all_to_all | solution.py:35
  23.1 2.4 %fusion.3 = bf16[1024,128]{0,1:T(8,128)(2,1)S(1)} fusion(bf16[1024,128]{1,0:T(8,128)(2,1)S(1)} %bitcast.38, bf16[1024,1024]{1,0:T(8,128)(2,1)} %param.15), kind=kOutput, calls=%fused_computation.10 | convolution fusion | flops 268566528 | bytes 2621440 | tf_op jit(solution)/shard_map/dot_general | solution.py:37
  25.5 0.8 %copy.27 = bf16[1024,128]{1,0:T(8,128)(2,1)} copy(bf16[1024,128]{0,1:T(8,128)(2,1)S(1)} %fusion.3) | data formatting | bytes 524288 | tf_op jit(solution)/shard_map/reshape | solution.py:40
  26.3 3.6 %all-to-all-start.1 = ((bf16[8,128,128]{2,1,0:T(8,128)(2,1)}), bf16[8,128,128]{2,1,0:T(8,128)(2,1)S(1)}, u32[]{:S(2)}, u32[]{:S(2)}) async-start(bf16[8,128,128]{2,1,0:T(8,128)(2,1)} %bitcast.3), calls=%async_computation.1 | async-start | bytes 524288 | tf_op jit(solution)/shard_map/all_to_all | solution.py:41
  29.9 42.2 %all-reduce.1 = bf16[256,128]{1,0:T(8,128)(2,1)} all-reduce(f32[256,128]{1,0:T(8,128)S(1)} %fusion.13), channel_id=1, replica_groups=mesh['row'=4,'col'=8] {'row','col'}, use_global_device_ids=true, to_apply=%region_1.3 | all-reduce | flops 32768 | bytes 196608 | tf_op jit(solution)/shard_map/psum | solution.py:60
  72.1 0.0 collective-permute-done
  72.1 1.0 %fusion.11 = (bf16[1,256,128]{2,1,0:T(8,128)(2,1)S(1)}, bf16[1,256,128]{2,1,0:T(8,128)(2,1)S(1)}) fusion(f32[2,256,128]{2,1,0:T(8,128)} %collective-permute-done, f32[2,256,128]{2,1,0:T(8,128)S(1)} %fusion.4), kind=kLoop, calls=%fused_computation.28 | loop fusion | flops 65536 | bytes 458752 | tf_op jit(solution)/shard_map/slice | solution.py:55
  73.1 2.3 %collective-permute-start.1 = (bf16[1,256,128]{2,1,0:T(8,128)(2,1)S(1)}, bf16[1,256,128]{2,1,0:T(8,128)(2,1)}, u32[]{:S(2)}, u32[]{:S(2)}) collective-permute-start(bf16[1,256,128]{2,1,0:T(8,128)(2,1)S(1)} %get-tuple-element.9), channel_id=1, source_target_pairs={{0,16},{8,24},{16,0},{24,8},{1,17},{9,25},{17,1},{25,9},{2,18},{10... | collective-permute-start | bytes 196616 | tf_op jit(solution)/shard_map/ppermute | solution.py:10
  75.5 0.0 all-to-all-done.1
  75.5 0.6 gather_fusion.1
  76.1 0.0 copy-start.1
  76.1 0.1 broadcast_select_fusion
  76.2 0.0 copy-start.2
  76.2 0.0 copy-start.3
  76.2 2.4 %fusion = f32[1024,128]{1,0:T(8,128)S(1)} fusion(f32[1024,128]{1,0:T(8,128)S(1)} %fusion.12, bf16[1024,1024]{1,0:T(8,128)(2,1)} %param.16, bf16[1024,128]{1,0:T(8,128)(2,1)S(1)} %bitcast.39), kind=kOutput, calls=%fused_computation.5 | convolution fusion | flops 268566528 | bytes 3407872 | tf_op jit(solution)/shard_map/dot_general | solution.py:43
  78.6 0.0 collective-permute-done.1
  78.6 0.0 copy-done.1
  78.6 1.3 %fusion.2 = f32[1024,128]{1,0:T(8,128)S(1)} fusion(f32[1024,128]{1,0:T(8,128)S(1)} %fusion, bf16[2,1024,256]{2,1,0:T(8,128)(2,1)S(1)} %copy-done.1, bf16[1,256,128]{2,1,0:T(8,128)(2,1)} %collective-permute-done.1, bf16[1,256,128]{2,1,0:T(8,128)(2,1)S(1)} %get-tuple-element.8), kind=kOutput, calls=%fused_computation.7 | convolution fusion | flops 134414336 | bytes 2228224 | tf_op jit(solution)/shard_map/blr,brw->lw/dot_general | solution.py:61
  79.9 0.0 copy-done.2
  79.9 0.0 copy-done.3
  79.9 1.1 %fusion.1 = f32[1024,128]{1,0:T(8,128)} fusion(f32[1024,128]{1,0:T(8,128)S(1)} %fusion.2, bf16[1024,256]{1,0:T(8,128)(2,1)S(1)} %copy-done.2, bf16[256,128]{1,0:T(8,128)(2,1)S(1)} %copy-done.3), kind=kOutput, calls=%fused_computation.6 | convolution fusion | flops 67239936 | bytes 1638400 | tf_op jit(solution)/shard_map/dot_general | solution.py:67
  (7 shorter events, 0.0 us)
Async XLA Ops:
  0.0 4.4 %copy-start = (bf16[1024,1024]{1,0:T(8,128)(2,1)S(1)}, bf16[1024,1024]{1,0:T(8,128)(2,1)}, u32[]{:S(2)}) copy-start(bf16[1024,1024]{1,0:T(8,128)(2,1)} %param.14) | copy-start | bytes 6291460
  0.0 3.5 %copy-start.4 = (s32[8]{0:T(128)S(1)}, s32[8]{0:T(128)}, u32[]{:S(2)}) copy-start(s32[8]{0:T(128)} %param.21) | copy-start | bytes 100
  2.9 69.2 %collective-permute-start = (f32[2,256,128]{2,1,0:T(8,128)S(1)}, f32[2,256,128]{2,1,0:T(8,128)}, u32[]{:S(2)}, u32[]{:S(2)}) collective-permute-start(f32[2,256,128]{2,1,0:T(8,128)S(1)} %fusion.4), channel_id=1, source_target_pairs={{0,8},{8,0},{16,24},{24,16},{1,9},{9,1},{17,25},{25,17},{2,10},{10... | collective-permute-start | bytes 786440 | tf_op jit(solution)/shard_map/ppermute | solution.py:10
  6.6 16.4 %all-to-all-start = ((bf16[8,128,128]{2,1,0:T(8,128)(2,1)}), bf16[8,128,128]{2,1,0:T(8,128)(2,1)S(1)}, u32[]{:S(2)}, u32[]{:S(2)}) async-start(bf16[8,128,128]{2,1,0:T(8,128)(2,1)} %broadcast_select_fusion.1), calls=%async_computation | async-start | bytes 524288 | tf_op jit(solution)/shard_map/all_to_all | solution.py:35
  26.3 49.2 %all-to-all-start.1 = ((bf16[8,128,128]{2,1,0:T(8,128)(2,1)}), bf16[8,128,128]{2,1,0:T(8,128)(2,1)S(1)}, u32[]{:S(2)}, u32[]{:S(2)}) async-start(bf16[8,128,128]{2,1,0:T(8,128)(2,1)} %bitcast.3), calls=%async_computation.1 | async-start | bytes 524288 | tf_op jit(solution)/shard_map/all_to_all | solution.py:41
  73.1 5.5 %collective-permute-start.1 = (bf16[1,256,128]{2,1,0:T(8,128)(2,1)S(1)}, bf16[1,256,128]{2,1,0:T(8,128)(2,1)}, u32[]{:S(2)}, u32[]{:S(2)}) collective-permute-start(bf16[1,256,128]{2,1,0:T(8,128)(2,1)S(1)} %get-tuple-element.9), channel_id=1, source_target_pairs={{0,16},{8,24},{16,0},{24,8},{1,17},{9,25},{17,1},{25,9},{2,18},{10... | collective-permute-start | bytes 196616 | tf_op jit(solution)/shard_map/ppermute | solution.py:10
  76.1 2.5 %copy-start.1 = (bf16[2,1024,256]{2,1,0:T(8,128)(2,1)S(1)}, bf16[2,1024,256]{2,1,0:T(8,128)(2,1)}, u32[]{:S(2)}) copy-start(bf16[2,1024,256]{2,1,0:T(8,128)(2,1)} %param.18) | copy-start | bytes 3145732
  76.2 3.7 %copy-start.2 = (bf16[1024,256]{1,0:T(8,128)(2,1)S(1)}, bf16[1024,256]{1,0:T(8,128)(2,1)}, u32[]{:S(2)}) copy-start(bf16[1024,256]{1,0:T(8,128)(2,1)} %param.20) | copy-start | bytes 1572868
  76.2 3.7 %copy-start.3 = (bf16[256,128]{1,0:T(8,128)(2,1)S(1)}, bf16[256,128]{1,0:T(8,128)(2,1)}, u32[]{:S(2)}) copy-start(bf16[256,128]{1,0:T(8,128)(2,1)} %all-reduce.1) | copy-start | bytes 196612
where the time goes:
time: 81.6 us; the launch traced here: 81 us
  blocking collectives  42.2 us (52%)
  matrix products  13.3 us (16%)
  starting transfers between devices  13.3 us (16%)
  waiting for transfers between devices  5.86 us (7%)
  other arithmetic  4.11 us (5%)
  local copies, waits for them, and re-layouts  2.06 us (3%)
    psum x1, blocking collectives, per_device(): root_sum = lax.psum(root_term, ('row', 'col'))  42.2 us
    all_to_all x1, starting transfers between devices, per_device(): lax.all_to_all(outgoing, 'col', split_axis=0, concat_axis=0, tiled=True)  6.86 us
    all_to_all x1, waiting for transfers between devices, per_device(): lax.all_to_all(outgoing, 'col', split_axis=0, concat_axis=0, tiled=True)  5.86 us
    all_to_all x1, starting transfers between devices, per_device(): lax.all_to_all(mixed_rows, 'col', split_axis=0, concat_axis=0, tiled=True)  3.59 us
    ppermute x2, starting transfers between devices, swapped(): lax.ppermute(x, axis, [(i, i ^ 1 << bit) for i in range(lax.axis_size(axi...  2.84 us
    dot_general x1, matrix products, per_device(): jnp.dot(middle, arrived.reshape(-1, shape_now[2]), preferred_element_type...  2.41 us
    dot_general x1, matrix products, per_device(): cluster_part = jnp.dot(expand, ordered, preferred_element_type=jnp.float32)  2.4 us
    dot_general x1, matrix products, per_device(): jnp.dot(leaf_inverse, lowered, preferred_element_type=jnp.float32)  2.3 us
  transfers between devices with their start and end apart: 4, of which 1 were waited for; matrix products, arithmetic and copies ran while one was open for 17% of the time, Pallas kernels for 0%

commit v1 on v0

v1 whole, which is shorter than its diff:
```python
import jax
import jax.numpy as jnp
from jax import lax
from jax.experimental import pallas as pl
from jax.experimental.pallas import tpu as pltpu
from jax.sharding import PartitionSpec as P

bf16 = jnp.bfloat16
f32 = jnp.float32
contract_first = (((0,), (0,)), ((), ()))
plain = (((1,), (0,)), ((), ()))
in_vmem = pl.BlockSpec(memory_space=pltpu.VMEM)
in_smem = pl.BlockSpec(memory_space=pltpu.SMEM)
in_hbm = pl.BlockSpec(memory_space=pltpu.HBM)
in_place = pl.BlockSpec(memory_space=pl.ANY)
limit = 24 * 1024 * 1024
waited = 10**10


def swapped(x, axis, bit):
    return lax.ppermute(x, axis, [(i, i ^ 1 << bit) for i in range(lax.axis_size(axis))])


def exchanged(x):
    return lax.all_to_all(x, "col", split_axis=0, concat_axis=0, tiled=True)


def ahead(x):
    return pltpu.with_memory_space_constraint(x, pltpu.VMEM)


def left(x):
    return pltpu.with_memory_space_constraint(x, pltpu.HBM)


def mul(a, b, dims=plain):
    return lax.dot_general(a, b, dims, preferred_element_type=f32)


def shape(dims, dtype):
    return jax.ShapeDtypeStruct(dims, dtype)


def call(kernel, out, args, specs=None, out_specs=None, scratch=(), aliases=None, flops=0, name=None):
    return pl.pallas_call(
        kernel,
        out_shape=out,
        in_specs=specs or [in_vmem] * len(args),
        out_specs=out_specs or jax.tree.map(lambda _: in_vmem, out),
        scratch_shapes=scratch,
        input_output_aliases=aliases or {},
        compiler_params=pltpu.CompilerParams(vmem_limit_bytes=limit),
        cost_estimate=pl.CostEstimate(flops=flops, bytes_accessed=flops // 256, transcendentals=0),
        name=name,
    )(*args)


def compress_kernel(
    owner_hbm, x_hbm, compress_hbm, root_hbm,
    low_ref, out_hbm, send_ref, keep_ref,
    owner_ref, x_ref, compress_ref, root_ref, product_ref, out_ref, sems, out_sems,
):
    pieces, size, _ = out_ref.shape
    width = 2 * size
    blocks = pieces // 2
    x_copy = pltpu.make_async_copy(x_hbm, x_ref, sems.at[0])
    owner_copy = pltpu.make_async_copy(owner_hbm, owner_ref, sems.at[1])
    root_copy = pltpu.make_async_copy(root_hbm, root_ref, sems.at[2])
    compress_copies = [
        pltpu.make_async_copy(
            compress_hbm.at[:, b * width : (b + 1) * width],
            compress_ref.at[:, b * width : (b + 1) * width],
            sems.at[3 + b],
        )
        for b in range(blocks)
    ]
    for copy in [x_copy, owner_copy, *compress_copies, root_copy]:
        copy.start()
    x_copy.wait()
    low_ref[...] = x_ref[...].astype(bf16)
    low = low_ref[...]
    owner_copy.wait()
    outs = []
    for b in range(blocks):
        compress_copies[b].wait()
        product = mul(compress_ref[:, b * width : (b + 1) * width], low, contract_first).astype(bf16)
        for k in (2 * b, 2 * b + 1):
            out_ref[k] = product[(k - 2 * b) * size : (k - 2 * b + 1) * size]
            outs.append(
                pltpu.make_async_copy(out_ref.at[k], out_hbm.at[owner_ref[k]], out_sems.at[k])
            )
            outs[-1].start()
    root_copy.wait()
    product_ref[...] = mul(root_ref[...], low, contract_first)
    half = keep_ref.shape[0]
    mine = lax.rem(lax.axis_index("row"), 2)
    keep_ref[...] = product_ref[pl.ds(pl.multiple_of(mine * half, half), half), :]
    send_ref[...] = product_ref[pl.ds(pl.multiple_of((1 - mine) * half, half), half), :].astype(bf16)
    for copy in outs:
        copy.wait()


def compressed(owner_map, x, compress, root_project):
    rows, columns = x.shape
    wide = compress.shape[1]
    pieces = owner_map.shape[0]
    rank = root_project.shape[1]
    outgoing = (pieces, wide // pieces, columns)
    return call(
        compress_kernel,
        [
            shape((rows, columns), bf16),
            shape(outgoing, bf16),
            shape((rank // 2, columns), bf16),
            shape((rank // 2, columns), f32),
        ],
        (left(owner_map), left(x), left(compress), left(root_project)),
        specs=[in_place] * 4,
        out_specs=[in_vmem, in_hbm, in_vmem, in_vmem],
        scratch=[
            pltpu.SMEM(owner_map.shape, jnp.int32),
            pltpu.VMEM((rows, columns), f32),
            pltpu.VMEM((rows, wide), bf16),
            pltpu.VMEM((rows, rank), bf16),
            pltpu.VMEM((rank, columns), f32),
            pltpu.VMEM(outgoing, bf16),
            pltpu.SemaphoreType.DMA((3 + pieces // 2,)),
            pltpu.SemaphoreType.DMA((pieces,)),
        ],
        flops=2 * rows * (wide + rank) * columns,
        name="compress",
    )


def split_kernel(keep_ref, got_ref, low_ref, own_ref, same_ref, other_ref, through_ref, total_ref):
    total_ref[...] = keep_ref[...] + got_ref[...].astype(f32)
    part = own_ref.shape[0]
    mine = lax.rem(lax.axis_index("col"), 2)
    own = total_ref[pl.ds(pl.multiple_of(mine * part, part), part), :]
    own_ref[...] = own
    same_ref[...] = own.astype(bf16)
    other_ref[...] = total_ref[pl.ds(pl.multiple_of((1 - mine) * part, part), part), :].astype(bf16)


def levels_kernel(low_ref, basis_hbm, out_ref, send_ref, basis_ref, sem):
    copy = pltpu.make_async_copy(basis_hbm, basis_ref, sem)
    copy.start()
    low = low_ref[...]
    copy.wait()
    for level in range(basis_ref.shape[0]):
        product = mul(basis_ref[level], low, contract_first)
        out_ref[level] = product
        send_ref[level] = product.astype(bf16)


def middle_kernel(middle_ref, arrived_ref, low_ref, running_ref, own_ref, *refs):
    got, (out_hbm, _, _, out_ref, sems) = refs[:-5], refs[-5:]
    pieces, size, columns = arrived_ref.shape
    total = own_ref[...]
    for got_ref in got:
        total += got_ref[...].astype(f32)
    part = total.astype(bf16)
    arrived = arrived_ref[...].reshape(pieces * size, columns)
    copies = []
    for b in range(0, pieces, 2):
        product = mul(middle_ref[b * size : (b + 2) * size, :], arrived).astype(bf16)
        for k in (b, b + 1):
            out_ref[k, :size] = product[(k - b) * size : (k - b + 1) * size]
            out_ref[k, size:] = part
            copies.append(pltpu.make_async_copy(out_ref.at[k], out_hbm.at[k], sems.at[k]))
            copies[-1].start()
    for copy in copies:
        copy.wait()


def add_kernel(keep_ref, got_ref, sum_ref, send_ref):
    total = keep_ref[...] + got_ref[...].astype(f32)
    sum_ref[...] = total
    send_ref[...] = total.astype(bf16)


def dense_kernel(
    owner_hbm, low_ref, inverse_hbm, row_hbm, expand_hbm, root_hbm,
    out_ref, row_ref, expand_ref, root_ref,
    owner_ref, inverse_ref, sems, expand_sems,
):
    owner_copy = pltpu.make_async_copy(owner_hbm, owner_ref, sems.at[0])
    inverse_copy = pltpu.make_async_copy(inverse_hbm, inverse_ref, sems.at[1])
    row_copy = pltpu.make_async_copy(row_hbm, row_ref, sems.at[2])
    root_copy = pltpu.make_async_copy(root_hbm, root_ref, sems.at[3])
    for copy in (owner_copy, inverse_copy, row_copy, root_copy):
        copy.start()
    owner_copy.wait()
    pieces = expand_sems.shape[0]
    size = expand_ref.shape[1] // pieces
    expand_copies = []
    for k in range(pieces):
        place = pl.ds(pl.multiple_of(owner_ref[k] * size, size), size)
        expand_copies.append(
            pltpu.make_async_copy(
                expand_hbm.at[:, k * size : (k + 1) * size], expand_ref.at[:, place], expand_sems.at[k]
            )
        )
        expand_copies[-1].start()
    inverse_copy.wait()
    out_ref[...] = mul(inverse_ref[...], low_ref[...])
    for copy in (row_copy, root_copy, *expand_copies):
        copy.wait()


def couple_kernel(dense_ref, expand_ref, *refs):
    out_ref = refs[-1]
    total = dense_ref[...]
    for level, sibling_ref in enumerate(refs[:-1]):
        total += mul(expand_ref[level], sibling_ref[...])
    out_ref[...] = total


def root_kernel(returned_ref, partial_ref, out_ref, through_ref):
    part = out_ref.shape[0] // 2
    size = returned_ref.shape[1] - part
    for parity in range(2):
        total = jnp.zeros((part, out_ref.shape[1]), f32)
        for d in range(parity, returned_ref.shape[0], 2):
            total += returned_ref[d, size:, :].astype(f32)
        out_ref[parity * part : (parity + 1) * part] = total.astype(bf16)


def expand_kernel(partial_ref, expand_ref, returned_ref, out_ref):
    pieces = returned_ref.shape[0]
    size = expand_ref.shape[1] // pieces
    returned = jnp.concatenate([returned_ref[k, :size] for k in range(pieces)], axis=0)
    out_ref[...] = partial_ref[...] + mul(expand_ref[...], returned)


def final_kernel(partial_ref, root_expand_ref, mine_ref, other_ref, out_ref, root_ref):
    half = mine_ref.shape[0]
    mine = lax.rem(lax.axis_index("row"), 2)
    root_ref[pl.ds(pl.multiple_of(mine * half, half), half), :] = mine_ref[...]
    root_ref[pl.ds(pl.multiple_of((1 - mine) * half, half), half), :] = other_ref[...]
    out_ref[...] = partial_ref[...] + mul(root_expand_ref[...], root_ref[...])


def per_device(
    right_side,
    leaf_inverse,
    compress,
    middle,
    expand,
    row_project,
    row_expand,
    root_project,
    root_expand,
    owner_map,
):
    rows, columns = right_side.shape
    levels, _, rank = row_project.shape
    row_count = lax.axis_size("row")
    col_count = lax.axis_size("col")
    half = rank // 2
    part = half // 2

    low, outgoing, send, keep = compressed(owner_map, right_side, compress, root_project)
    got = swapped(send, "row", 0)
    arrived = exchanged(outgoing)
    own, same, other, low = call(
        split_kernel,
        [
            shape((part, columns), f32),
            shape((part, columns), bf16),
            shape((part, columns), bf16),
            shape(low.shape, bf16),
        ],
        (keep, got, low),
        scratch=[pltpu.VMEM((half, columns), f32)],
        aliases={2: 3},
        flops=waited,
        name="root_split",
    )
    parts = []
    for row_step in range(0, row_count, 2):
        for col_step in range(2):
            if row_step or col_step:
                pairs = [
                    (r * col_count + c, (r ^ row_step) * col_count + (c ^ col_step))
                    for r in range(row_count)
                    for c in range(col_count)
                ]
                parts.append(lax.ppermute(other if col_step else same, ("row", "col"), pairs))
    running, level_send = call(
        levels_kernel,
        [shape((levels, rank, columns), f32), shape((levels, rank, columns), bf16)],
        (low, left(row_project)),
        specs=[in_vmem, in_place],
        scratch=[pltpu.VMEM(row_project.shape, bf16), pltpu.SemaphoreType.DMA],
        flops=2 * rows * rank * levels * columns,
        name="levels",
    )
    partner = swapped(level_send, "row", 0)

    size = middle.shape[0] // col_count
    mixed_shape = (col_count, size + part, columns)
    mixed, low, running = call(
        middle_kernel,
        [shape(mixed_shape, bf16), shape(low.shape, bf16), shape(running.shape, f32)],
        (ahead(middle), arrived, low, running, own, *parts),
        out_specs=[in_hbm, in_vmem, in_vmem],
        scratch=[pltpu.VMEM(mixed_shape, bf16), pltpu.SemaphoreType.DMA((col_count,))],
        aliases={2: 1, 3: 2},
        flops=2 * middle.shape[0] * middle.shape[1] * columns,
        name="middle",
    )
    returned = exchanged(mixed)

    dense, row_expand, expand, root_expand = call(
        dense_kernel,
        [
            shape((rows, columns), f32),
            pltpu.VMEM(row_expand.shape, bf16),
            pltpu.VMEM(expand.shape, bf16),
            pltpu.VMEM(root_expand.shape, bf16),
        ],
        (left(owner_map), low, left(leaf_inverse), left(row_expand), left(expand), left(root_expand)),
        specs=[in_place, in_vmem] + [in_place] * 4,
        scratch=[
            pltpu.SMEM(owner_map.shape, jnp.int32),
            pltpu.VMEM(leaf_inverse.shape, bf16),
            pltpu.SemaphoreType.DMA((4,)),
            pltpu.SemaphoreType.DMA((col_count,)),
        ],
        flops=2 * rows * rows * columns,
        name="dense",
    )
    siblings = [partner[0]]
    for bit in range(1, levels):
        running, level_send = call(
            add_kernel,
            [shape(running[1:].shape, f32), shape(running[1:].shape, bf16)],
            (running[1:], partner[1:]),
            name="level_sum",
        )
        partner = swapped(level_send, "row", bit)
        siblings.append(partner[0])
    partial = call(
        couple_kernel,
        shape((rows, columns), f32),
        (dense, row_expand, *siblings),
        flops=2 * rows * rank * levels * columns,
        name="couple",
    )

    root_mine, partial = call(
        root_kernel,
        [shape((half, columns), bf16), shape(partial.shape, f32)],
        (returned, partial),
        aliases={1: 1},
        name="root_sum",
    )
    root_other = swapped(root_mine, "row", 0)
    partial = call(
        expand_kernel,
        shape((rows, columns), f32),
        (partial, expand, returned),
        flops=2 * rows * expand.shape[1] * columns,
        name="expand",
    )
    return call(
        final_kernel,
        shape((rows, columns), f32),
        (partial, root_expand, root_mine, root_other),
        scratch=[pltpu.VMEM((rank, columns), bf16)],
        flops=2 * rows * rank * columns,
        name="final",
    )


def solution(mesh):
    leaves = P(("row", "col"), None)
    levels = P(None, ("row", "col"), None)
    return jax.shard_map(
        per_device,
        mesh=mesh,
        in_specs=(leaves,) * 5 + (levels,) * 2 + (leaves,) * 2 + (P(),),
        out_specs=leaves,
        check_vma=False,
    )
```

time: 81.6 us -> 40 us (0.49)
  blocking collectives: 42.2 us -> 0 us
  matrix products: 13.3 us -> 0 us
  Pallas kernels: 0 us -> 12.4 us
  waiting for transfers between devices: 5.86 us -> 11 us
  other arithmetic: 4.11 us -> 0 us
  starting transfers between devices: 13.3 us -> 16.1 us
  local copies, waits for them, and re-layouts: 2.06 us -> 0.03 us
    psum x1 -> x0, blocking collectives: 42.2 us -> none  [per_device(): root_sum = lax.psum(root_term, ('row', 'col'))]
    dot_general x8 -> x0, matrix products: 13.3 us -> none  [the longest x1 2.41 us: per_device(): jnp.dot(middle, arrived.reshape(-1, shape_now[2]), preferred_element_type...]
    pallas_call x0 -> x10, Pallas kernels: none -> 12.4 us  [call(): pl.pallas_call(kernel, out_shape=out, in_specs=specs or [in_vmem] * len(a...]
    ppermute x0 -> x3, starting transfers between devices: none -> 3.57 us  [per_device(): lax.ppermute(other if col_step else same, ('row', 'col'), pairs)]
    ppermute x0 -> x3, waiting for transfers between devices: none -> 2.05 us  [per_device(): lax.ppermute(other if col_step else same, ('row', 'col'), pairs)]
    ppermute x2 -> x4, waiting for transfers between devices: 0.01 us -> 1.82 us  [swapped(): lax.ppermute(x, axis, [(i, i ^ 1 << bit) for i in range(lax.axis_size(axi...]
    all_to_all x2, waiting for transfers between devices: 5.86 us -> 7.15 us  [exchanged(): return lax.all_to_all(x, 'col', split_axis=0, concat_axis=0, tiled=True)]
    convert_element_type x1 -> x0, other arithmetic: 1.23 us -> none  [per_device(): lowered = right_side.astype(jnp.bfloat16)]
  transfers between devices with their start and end apart: 4 -> 9, of which waited for: 1 -> 6; matrix products, arithmetic and copies ran while one was open for 17% -> 0% of each run, Pallas kernels for 0% -> 16%
where the time goes in v1:
time: 40 us; the launch traced here: 39.6 us
  starting transfers between devices  16.1 us (40%)
  Pallas kernels  12.4 us (31%)
  waiting for transfers between devices  11 us (28%)
    pallas_call x10, Pallas kernels, call(): pl.pallas_call(kernel, out_shape=out, in_specs=specs or [in_vmem] * len(a...  12.4 us
    all_to_all x2, starting transfers between devices, exchanged(): return lax.all_to_all(x, 'col', split_axis=0, concat_axis=0, tiled=True)  10.5 us
    all_to_all x2, waiting for transfers between devices, exchanged(): return lax.all_to_all(x, 'col', split_axis=0, concat_axis=0, tiled=True)  7.15 us
    ppermute x3, starting transfers between devices, per_device(): lax.ppermute(other if col_step else same, ('row', 'col'), pairs)  3.57 us
    ppermute x4, starting transfers between devices, swapped(): lax.ppermute(x, axis, [(i, i ^ 1 << bit) for i in range(lax.axis_size(axi...  2.08 us
    ppermute x3, waiting for transfers between devices, per_device(): lax.ppermute(other if col_step else same, ('row', 'col'), pairs)  2.05 us
    ppermute x4, waiting for transfers between devices, swapped(): lax.ppermute(x, axis, [(i, i ^ 1 << bit) for i in range(lax.axis_size(axi...  1.82 us
  transfers between devices with their start and end apart: 9, of which 6 were waited for; matrix products, arithmetic and copies ran while one was open for 0% of the time, Pallas kernels for 16%

profile of v1, /device:TPU:0, one launch (start us, length us, event | category | flops | bytes accessed | tf_op | source)
XLA Modules:
  0.0 39.6 jit_solution(7427529869269868104)
XLA Ops:
  0.0 3.4 %compress.1 = (bf16[1024,128]{1,0:T(8,128)(2,1)S(1)}, bf16[8,128,128]{2,1,0:T(8,128)(2,1)}, bf16[128,128]{1,0:T(8,128)(2,1)S(1)}, f32[128,128]{1,0:T(8,128)S(1)}) custom-call(s32[8]{0:T(128)} %owner_hbm.3, f32[1024,128]{1,0:T(8,128)} %x_hbm.1, bf16[1024,1024]{1,0:T(8,128)(2,1)} %compress_hbm.1, bf16[1024,256]{1,0:T(8,128)(2,1)} %root_hbm.2), custom_call_target="tpu_custom_call" | custom-call | flops 335544320 | bytes 1310720 | tf_op jit(solution)/shard_map/compress/pallas_call | solution.py:45
  3.4 0.5 %collective-permute-start = (bf16[128,128]{1,0:T(8,128)(2,1)S(1)}, bf16[128,128]{1,0:T(8,128)(2,1)S(1)}, u32[]{:S(2)}, u32[]{:S(2)}) collective-permute-start(bf16[128,128]{1,0:T(8,128)(2,1)S(1)} %get-tuple-element.27), channel_id=1, source_target_pairs={{0,8},{8,0},{16,24},{24,16},{1,9},{9,1},{17,25},{25,17},{2,10},{10... | collective-permute-start | bytes 98312 | tf_op jit(solution)/shard_map/ppermute | solution.py:21
  3.9 6.9 %all-to-all-start = ((bf16[8,128,128]{2,1,0:T(8,128)(2,1)}), bf16[8,128,128]{2,1,0:T(8,128)(2,1)S(1)}, u32[]{:S(2)}, u32[]{:S(2)}) async-start(bf16[8,128,128]{2,1,0:T(8,128)(2,1)} %get-tuple-element.25), calls=%async_computation | async-start | bytes 524288 | tf_op jit(solution)/shard_map/all_to_all | solution.py:25
  10.8 0.0 collective-permute-done.got_ref
  10.8 0.0 copy-start
  10.8 1.6 %collective-permute-start.2 = (bf16[64,128]{1,0:T(8,128)(2,1)S(1)}, bf16[64,128]{1,0:T(8,128)(2,1)S(1)}, u32[]{:S(2)}, u32[]{:S(2)}) collective-permute-start(bf16[64,128]{1,0:T(8,128)(2,1)S(1)} %get-tuple-element.33), channel_id=1, source_target_pairs={{0,16},{1,17},{2,18},{3,19},{4,20},{5,21},{6,22},{7,23},{8,24},{9,... | collective-permute-start | bytes 49160 | tf_op jit(solution)/shard_map/ppermute | solution.py:289
  12.4 2.0 %collective-permute-start.3 = (bf16[64,128]{1,0:T(8,128)(2,1)S(1)}, bf16[64,128]{1,0:T(8,128)(2,1)S(1)}, u32[]{:S(2)}, u32[]{:S(2)}) collective-permute-start(bf16[64,128]{1,0:T(8,128)(2,1)S(1)} %get-tuple-element.32), channel_id=1, source_target_pairs={{0,17},{1,16},{2,19},{3,18},{4,21},{5,20},{6,23},{7,22},{8,25},{9,... | collective-permute-start | bytes 49160 | tf_op jit(solution)/shard_map/ppermute | solution.py:289
  14.4 0.0 collective-permute-start.1
  14.4 1.7 %levels.1 = (f32[2,256,128]{2,1,0:T(8,128)S(1)}, bf16[2,256,128]{2,1,0:T(8,128)(2,1)S(1)}) custom-call(bf16[1024,128]{1,0:T(8,128)(2,1)S(1)} %get-tuple-element.29.low_ref, bf16[2,1024,256]{2,1,0:T(8,128)(2,1)} %basis_hbm.1), custom_call_target="tpu_custom_call" | custom-call | flops 134217728 | bytes 524288 | tf_op jit(solution)/shard_map/levels/pallas_call | solution.py:45
  16.1 0.0 collective-permute-done.2.refs_1_
  16.1 1.0 %collective-permute-done.3.refs_2_ = bf16[64,128]{1,0:T(8,128)(2,1)S(1)} collective-permute-done((bf16[64,128]{1,0:T(8,128)(2,1)S(1)}, bf16[64,128]{1,0:T(8,128)(2,1)S(1)}, u32[]{:S(2)}, u32[]{:S(2)}) %collective-permute-start.3) | collective-permute-done | bytes 16416 | tf_op jit(solution)/shard_map/ppermute | solution.py:289
  17.1 1.1 %collective-permute-done.1.refs_0_ = bf16[64,128]{1,0:T(8,128)(2,1)S(1)} collective-permute-done((bf16[64,128]{1,0:T(8,128)(2,1)S(1)}, bf16[64,128]{1,0:T(8,128)(2,1)S(1)}, u32[]{:S(2)}, u32[]{:S(2)}) %collective-permute-start.1) | collective-permute-done | bytes 16416 | tf_op jit(solution)/shard_map/ppermute | solution.py:289
  18.2 2.2 %all-to-all-done.arrived_ref = bf16[8,128,128]{2,1,0:T(8,128)(2,1)S(1)} async-done(((bf16[8,128,128]{2,1,0:T(8,128)(2,1)}), bf16[8,128,128]{2,1,0:T(8,128)(2,1)S(1)}, u32[]{:S(2)}, u32[]{:S(2)}) %all-to-all-start) | async-done | bytes 262176 | tf_op jit(solution)/shard_map/all_to_all | solution.py:25
  20.4 0.0 copy-done
  20.4 1.4 %middle.1 = (bf16[8,192,128]{2,1,0:T(8,128)(2,1)}, bf16[1024,128]{1,0:T(8,128)(2,1)S(1)}, f32[2,256,128]{2,1,0:T(8,128)S(1)}) custom-call(bf16[1024,1024]{1,0:T(8,128)(2,1)S(1)} %copy-done, bf16[8,128,128]{2,1,0:T(8,128)(2,1)S(1)} %all-to-all-done.arrived_ref, ...), custom_call_target="tpu_custom_call", output_to_operand_aliasing={{1}: (2, {}), {2}: (3, {})} | custom-call | flops 268435456 | bytes 1048576 | tf_op jit(solution)/shard_map/middle/pallas_call | solution.py:45
  21.8 3.6 %all-to-all-start.1 = ((bf16[8,192,128]{2,1,0:T(8,128)(2,1)}), bf16[8,192,128]{2,1,0:T(8,128)(2,1)S(1)}, u32[]{:S(2)}, u32[]{:S(2)}) async-start(bf16[8,192,128]{2,1,0:T(8,128)(2,1)} %get-tuple-element.34), calls=%async_computation.1 | async-start | bytes 786432 | tf_op jit(solution)/shard_map/all_to_all | solution.py:25
  25.4 0.0 collective-permute-start.4
  25.4 1.3 %collective-permute-done.4 = bf16[2,256,128]{2,1,0:T(8,128)(2,1)S(1)} collective-permute-done((bf16[2,256,128]{2,1,0:T(8,128)(2,1)S(1)}, bf16[2,256,128]{2,1,0:T(8,128)(2,1)S(1)}, u32[]{:S(2)}, u32[]{:S(2)}) %collective-permute-start.4) | collective-permute-done | bytes 131104 | tf_op jit(solution)/shard_map/ppermute | solution.py:21
  26.7 0.7 %level_sum.1 = (f32[1,256,128]{2,1,0:T(8,128)}, bf16[1,256,128]{2,1,0:T(8,128)(2,1)S(1)}) custom-call(f32[1,256,128]{2,1,0:T(8,128)S(1)} %slice.10.keep_ref, bf16[1,256,128]{2,1,0:T(8,128)(2,1)S(1)} %get-tuple-element.45.got_ref), custom_call_target="tpu_custom_call" | custom-call | tf_op jit(solution)/shard_map/level_sum/pallas_call | solution.py:45
  27.4 1.5 %collective-permute-start.5 = (bf16[1,256,128]{2,1,0:T(8,128)(2,1)S(1)}, bf16[1,256,128]{2,1,0:T(8,128)(2,1)S(1)}, u32[]{:S(2)}, u32[]{:S(2)}) collective-permute-start(bf16[1,256,128]{2,1,0:T(8,128)(2,1)S(1)} %get-tuple-element.40), channel_id=1, source_target_pairs={{0,16},{8,24},{16,0},{24,8},{1,17},{9,25},{17,1},{25,9},{2,18},{10... | collective-permute-start | bytes 196616 | tf_op jit(solution)/shard_map/ppermute | solution.py:21
  28.9 2.9 %dense.1 = (f32[1024,128]{1,0:T(8,128)S(1)}, bf16[2,1024,256]{2,1,0:T(8,128)(2,1)S(1)}, bf16[1024,1024]{1,0:T(8,128)(2,1)S(1)}, bf16[1024,256]{1,0:T(8,128)(2,1)S(1)}) custom-call(s32[8]{0:T(128)} %owner_hbm.3, bf16[1024,128]{1,0:T(8,128)(2,1)S(1)} %get-tuple-element.35.low_ref, bf16[1024,1024]{1,0:T(8,128)(2,1)} %inverse_hbm.1, ...), custom_call_target="tpu_custom_call" | custom-call | flops 268435456 | bytes 1048576 | tf_op jit(solution)/shard_map/dense/pallas_call | solution.py:45
  31.8 0.0 collective-permute-done.5
  31.8 0.4 %couple.1.partial_ref = f32[1024,128]{1,0:T(8,128)S(1)} custom-call(f32[1024,128]{1,0:T(8,128)S(1)} %get-tuple-element.36.dense_ref, bf16[2,1024,256]{2,1,0:T(8,128)(2,1)S(1)} %get-tuple-element.37.expand_ref, bf16[256,128]{1,0:T(8,128)(2,1)S(1)} %get-tuple-element.46.refs_0_, bf16[256,128]{1,0:T(8,128)(2,1)S(1)} %bitcast.3), custom_call_target="tpu_custom_call" | custom-call | flops 134217728 | bytes 524288 | tf_op jit(solution)/shard_map/couple/pallas_call | solution.py:45
  32.3 5.0 %all-to-all-done.1.returned_ref = bf16[8,192,128]{2,1,0:T(8,128)(2,1)S(1)} async-done(((bf16[8,192,128]{2,1,0:T(8,128)(2,1)}), bf16[8,192,128]{2,1,0:T(8,128)(2,1)S(1)}, u32[]{:S(2)}, u32[]{:S(2)}) %all-to-all-start.1) | async-done | bytes 393248 | tf_op jit(solution)/shard_map/all_to_all | solution.py:25
  37.3 0.1 collective-permute-start.6
  37.3 0.7 %expand.1.partial_ref = f32[1024,128]{1,0:T(8,128)S(1)} custom-call(f32[1024,128]{1,0:T(8,128)S(1)} %get-tuple-element.41.partial_ref, bf16[1024,1024]{1,0:T(8,128)(2,1)S(1)} %get-tuple-element.42.expand_ref, bf16[8,192,128]{2,1,0:T(8,128)(2,1)S(1)} %all-to-all-done.1.returned_ref), custom_call_target="tpu_custom_call" | custom-call | flops 268435456 | bytes 1048576 | tf_op jit(solution)/shard_map/expand/pallas_call | solution.py:45
  38.1 0.5 %collective-permute-done.6.other_ref = bf16[128,128]{1,0:T(8,128)(2,1)S(1)} collective-permute-done((bf16[128,128]{1,0:T(8,128)(2,1)S(1)}, bf16[128,128]{1,0:T(8,128)(2,1)S(1)}, u32[]{:S(2)}, u32[]{:S(2)}) %collective-permute-start.6) | collective-permute-done | bytes 32800 | tf_op jit(solution)/shard_map/ppermute | solution.py:21
  38.5 1.1 %final.1 = f32[1024,128]{1,0:T(8,128)} custom-call(f32[1024,128]{1,0:T(8,128)S(1)} %expand.1.partial_ref, bf16[1024,256]{1,0:T(8,128)(2,1)S(1)} %get-tuple-element.43.root_expand_ref, bf16[128,128]{1,0:T(8,128)(2,1)S(1)} %get-tuple-element.44.mine_ref, bf16[128,128]{1,0:T(8,128)(2,1)S(1)} %collective-permute-done.6.other_ref), custom_call_target="tpu_custom_call" | custom-call | flops 67108864 | bytes 262144 | tf_op jit(solution)/shard_map/final/pallas_call | solution.py:45
  (4 shorter events, 0.1 us)
Async XLA Ops:
  3.4 7.4 %collective-permute-start = (bf16[128,128]{1,0:T(8,128)(2,1)S(1)}, bf16[128,128]{1,0:T(8,128)(2,1)S(1)}, u32[]{:S(2)}, u32[]{:S(2)}) collective-permute-start(bf16[128,128]{1,0:T(8,128)(2,1)S(1)} %get-tuple-element.27), channel_id=1, source_target_pairs={{0,8},{8,0},{16,24},{24,16},{1,9},{9,1},{17,25},{25,17},{2,10},{10... | collective-permute-start | bytes 98312 | tf_op jit(solution)/shard_map/ppermute | solution.py:21
  3.9 16.4 %all-to-all-start = ((bf16[8,128,128]{2,1,0:T(8,128)(2,1)}), bf16[8,128,128]{2,1,0:T(8,128)(2,1)S(1)}, u32[]{:S(2)}, u32[]{:S(2)}) async-start(bf16[8,128,128]{2,1,0:T(8,128)(2,1)} %get-tuple-element.25), calls=%async_computation | async-start | bytes 524288 | tf_op jit(solution)/shard_map/all_to_all | solution.py:25
  10.8 9.6 %copy-start = (bf16[1024,1024]{1,0:T(8,128)(2,1)S(1)}, bf16[1024,1024]{1,0:T(8,128)(2,1)}, u32[]{:S(2)}) copy-start(bf16[1024,1024]{1,0:T(8,128)(2,1)} %middle_ref.1) | copy-start | bytes 6291460
  10.8 5.3 %collective-permute-start.2 = (bf16[64,128]{1,0:T(8,128)(2,1)S(1)}, bf16[64,128]{1,0:T(8,128)(2,1)S(1)}, u32[]{:S(2)}, u32[]{:S(2)}) collective-permute-start(bf16[64,128]{1,0:T(8,128)(2,1)S(1)} %get-tuple-element.33), channel_id=1, source_target_pairs={{0,16},{1,17},{2,18},{3,19},{4,20},{5,21},{6,22},{7,23},{8,24},{9,... | collective-permute-start | bytes 49160 | tf_op jit(solution)/shard_map/ppermute | solution.py:289
  12.4 4.7 %collective-permute-start.3 = (bf16[64,128]{1,0:T(8,128)(2,1)S(1)}, bf16[64,128]{1,0:T(8,128)(2,1)S(1)}, u32[]{:S(2)}, u32[]{:S(2)}) collective-permute-start(bf16[64,128]{1,0:T(8,128)(2,1)S(1)} %get-tuple-element.32), channel_id=1, source_target_pairs={{0,17},{1,16},{2,19},{3,18},{4,21},{5,20},{6,23},{7,22},{8,25},{9,... | collective-permute-start | bytes 49160 | tf_op jit(solution)/shard_map/ppermute | solution.py:289
  14.4 3.8 %collective-permute-start.1 = (bf16[64,128]{1,0:T(8,128)(2,1)S(1)}, bf16[64,128]{1,0:T(8,128)(2,1)S(1)}, u32[]{:S(2)}, u32[]{:S(2)}) collective-permute-start(bf16[64,128]{1,0:T(8,128)(2,1)S(1)} %get-tuple-element.32), channel_id=1, source_target_pairs={{0,1},{1,0},{2,3},{3,2},{4,5},{5,4},{6,7},{7,6},{8,9},{9,8},{10,11... | collective-permute-start | bytes 49160 | tf_op jit(solution)/shard_map/ppermute | solution.py:289
  21.8 15.5 %all-to-all-start.1 = ((bf16[8,192,128]{2,1,0:T(8,128)(2,1)}), bf16[8,192,128]{2,1,0:T(8,128)(2,1)S(1)}, u32[]{:S(2)}, u32[]{:S(2)}) async-start(bf16[8,192,128]{2,1,0:T(8,128)(2,1)} %get-tuple-element.34), calls=%async_computation.1 | async-start | bytes 786432 | tf_op jit(solution)/shard_map/all_to_all | solution.py:25
  25.4 1.3 %collective-permute-start.4 = (bf16[2,256,128]{2,1,0:T(8,128)(2,1)S(1)}, bf16[2,256,128]{2,1,0:T(8,128)(2,1)S(1)}, u32[]{:S(2)}, u32[]{:S(2)}) collective-permute-start(bf16[2,256,128]{2,1,0:T(8,128)(2,1)S(1)} %get-tuple-element.38), channel_id=1, source_target_pairs={{0,8},{8,0},{16,24},{24,16},{1,9},{9,1},{17,25},{25,17},{2,10},{10... | collective-permute-start | bytes 393224 | tf_op jit(solution)/shard_map/ppermute | solution.py:21
  27.4 4.4 %collective-permute-start.5 = (bf16[1,256,128]{2,1,0:T(8,128)(2,1)S(1)}, bf16[1,256,128]{2,1,0:T(8,128)(2,1)S(1)}, u32[]{:S(2)}, u32[]{:S(2)}) collective-permute-start(bf16[1,256,128]{2,1,0:T(8,128)(2,1)S(1)} %get-tuple-element.40), channel_id=1, source_target_pairs={{0,16},{8,24},{16,0},{24,8},{1,17},{9,25},{17,1},{25,9},{2,18},{10... | collective-permute-start | bytes 196616 | tf_op jit(solution)/shard_map/ppermute | solution.py:21
  37.3 1.3 %collective-permute-start.6 = (bf16[128,128]{1,0:T(8,128)(2,1)S(1)}, bf16[128,128]{1,0:T(8,128)(2,1)S(1)}, u32[]{:S(2)}, u32[]{:S(2)}) collective-permute-start(bf16[128,128]{1,0:T(8,128)(2,1)S(1)} %get-tuple-element.44.mine_ref), channel_id=1, source_target_pairs={{0,8},{8,0},{16,24},{24,16},{1,9},{9,1},{17,25},{25,17},{2,10},{10... | collective-permute-start | bytes 98312 | tf_op jit(solution)/shard_map/ppermute | solution.py:21

commit v2 on v1

--- a/solution.py
+++ b/solution.py
@@ -21,8 +21,21 @@
     return lax.ppermute(x, axis, [(i, i ^ 1 << bit) for i in range(lax.axis_size(axis))])
 
 
+def slots(count):
+    block = count // 4
+    return [quarter * block + i for quarter in (2, 0, 1, 3) for i in range(block)]
+
+
+def slot_of(device, count):
+    block = count // 4
+    quarter = device // block
+    moved = jnp.where(quarter == 3, 3, jnp.where(quarter == 2, 0, quarter + 1))
+    return device + (moved - quarter) * block
+
+
 def exchanged(x):
-    return lax.all_to_all(x, "col", split_axis=0, concat_axis=0, tiled=True)
+    groups = [slots(lax.axis_size("col"))]
+    return lax.all_to_all(x, "col", 0, 0, tiled=True, axis_index_groups=groups)
 
 
 def ahead(x):
@@ -58,11 +71,12 @@
 def compress_kernel(
     owner_hbm, x_hbm, compress_hbm, root_hbm,
     low_ref, out_hbm, send_ref, keep_ref,
-    owner_ref, x_ref, compress_ref, root_ref, product_ref, out_ref, sems, out_sems,
+    owner_ref, x_ref, compress_ref, root_ref, product_ref, out_ref, sems, compress_sems, out_sems,
 ):
     pieces, size, _ = out_ref.shape
-    width = 2 * size
-    blocks = pieces // 2
+    blocks = compress_sems.shape[0]
+    count = pieces // blocks
+    width = count * size
     x_copy = pltpu.make_async_copy(x_hbm, x_ref, sems.at[0])
     owner_copy = pltpu.make_async_copy(owner_hbm, owner_ref, sems.at[1])
     root_copy = pltpu.make_async_copy(root_hbm, root_ref, sems.at[2])
@@ -70,7 +84,7 @@
         pltpu.make_async_copy(
             compress_hbm.at[:, b * width : (b + 1) * width],
             compress_ref.at[:, b * width : (b + 1) * width],
-            sems.at[3 + b],
+            compress_sems.at[b],
         )
         for b in range(blocks)
     ]
@@ -79,15 +93,16 @@
     x_copy.wait()
     low_ref[...] = x_ref[...].astype(bf16)
     low = low_ref[...]
+    flat = low.T
     owner_copy.wait()
     outs = []
     for b in range(blocks):
         compress_copies[b].wait()
-        product = mul(compress_ref[:, b * width : (b + 1) * width], low, contract_first).astype(bf16)
-        for k in (2 * b, 2 * b + 1):
-            out_ref[k] = product[(k - 2 * b) * size : (k - 2 * b + 1) * size]
+        product = mul(flat, compress_ref[:, b * width : (b + 1) * width]).astype(bf16).T
+        out_ref[b * count : (b + 1) * count] = product.reshape(count, size, -1)
+        for k in range(b * count, (b + 1) * count):
             outs.append(
-                pltpu.make_async_copy(out_ref.at[k], out_hbm.at[owner_ref[k]], out_sems.at[k])
+                pltpu.make_async_copy(out_ref.at[k], out_hbm.at[slot_of(owner_ref[k], pieces)], out_sems.at[k])
             )
             outs[-1].start()
     root_copy.wait()
@@ -124,7 +139,8 @@
             pltpu.VMEM((rows, rank), bf16),
             pltpu.VMEM((rank, columns), f32),
             pltpu.VMEM(outgoing, bf16),
-            pltpu.SemaphoreType.DMA((3 + pieces // 2,)),
+            pltpu.SemaphoreType.DMA((3,)),
+            pltpu.SemaphoreType.DMA((2,)),
             pltpu.SemaphoreType.DMA((pieces,)),
         ],
         flops=2 * rows * (wide + rank) * columns,
@@ -160,15 +176,14 @@
     for got_ref in got:
         total += got_ref[...].astype(f32)
     part = total.astype(bf16)
-    arrived = arrived_ref[...].reshape(pieces * size, columns)
+    order = slots(pieces)
+    arrived = jnp.concatenate([arrived_ref[order.index(c)] for c in range(pieces)], axis=0)
     copies = []
-    for b in range(0, pieces, 2):
-        product = mul(middle_ref[b * size : (b + 2) * size, :], arrived).astype(bf16)
-        for k in (b, b + 1):
-            out_ref[k, :size] = product[(k - b) * size : (k - b + 1) * size]
-            out_ref[k, size:] = part
-            copies.append(pltpu.make_async_copy(out_ref.at[k], out_hbm.at[k], sems.at[k]))
-            copies[-1].start()
+    for k in range(pieces):
+        out_ref[k, :size] = mul(middle_ref[k * size : (k + 1) * size, :], arrived).astype(bf16)
+        out_ref[k, size:] = part
+        copies.append(pltpu.make_async_copy(out_ref.at[k], out_hbm.at[order.index(k)], sems.at[k]))
+        copies[-1].start()
     for copy in copies:
         copy.wait()
 
@@ -195,7 +210,7 @@
     size = expand_ref.shape[1] // pieces
     expand_copies = []
     for k in range(pieces):
-        place = pl.ds(pl.multiple_of(owner_ref[k] * size, size), size)
+        place = pl.ds(pl.multiple_of(slot_of(owner_ref[k], pieces) * size, size), size)
         expand_copies.append(
             pltpu.make_async_copy(
                 expand_hbm.at[:, k * size : (k + 1) * size], expand_ref.at[:, place], expand_sems.at[k]
@@ -219,10 +234,12 @@
 def root_kernel(returned_ref, partial_ref, out_ref, through_ref):
     part = out_ref.shape[0] // 2
     size = returned_ref.shape[1] - part
+    order = slots(returned_ref.shape[0])
     for parity in range(2):
         total = jnp.zeros((part, out_ref.shape[1]), f32)
-        for d in range(parity, returned_ref.shape[0], 2):
-            total += returned_ref[d, size:, :].astype(f32)
+        for k in range(returned_ref.shape[0]):
+            if order[k] % 2 == parity:
+                total += returned_ref[k, size:, :].astype(f32)
         out_ref[parity * part : (parity + 1) * part] = total.astype(bf16)
 
 

time: 40 us -> 36.1 us (0.903)
  waiting for transfers between devices: 11 us -> 6.34 us
  starting transfers between devices: 16.1 us -> 17.3 us
  Pallas kernels: 12.4 us -> 11.9 us
    all_to_all x2, waiting for transfers between devices: 7.15 us -> 3.06 us  [exchanged(): return lax.all_to_all(x, 'col', 0, 0, tiled=True, axis_index_groups=groups)]
    all_to_all x2, starting transfers between devices: 10.5 us -> 11.7 us  [exchanged(): return lax.all_to_all(x, 'col', 0, 0, tiled=True, axis_index_groups=groups)]
    ppermute x3, waiting for transfers between devices: 2.05 us -> 1.45 us  [per_device(): lax.ppermute(other if col_step else same, ('row', 'col'), pairs)]
    pallas_call x10, Pallas kernels: 12.4 us -> 11.9 us  [call(): pl.pallas_call(kernel, out_shape=out, in_specs=specs or [in_vmem] * len(a...]
  transfers between devices with their start and end apart: 9 -> 9, of which waited for: 6 -> 6; matrix products, arithmetic and copies ran while one was open for 0% -> 0% of each run, Pallas kernels for 16% -> 18%
where the time goes in v2:
time: 36.1 us; the launch traced here: 35.7 us
  starting transfers between devices  17.3 us (48%)
  Pallas kernels  11.9 us (33%)
  waiting for transfers between devices  6.34 us (18%)
    pallas_call x10, Pallas kernels, call(): pl.pallas_call(kernel, out_shape=out, in_specs=specs or [in_vmem] * len(a...  11.9 us
    all_to_all x2, starting transfers between devices, exchanged(): return lax.all_to_all(x, 'col', 0, 0, tiled=True, axis_index_groups=groups)  11.7 us
    ppermute x3, starting transfers between devices, per_device(): lax.ppermute(other if col_step else same, ('row', 'col'), pairs)  3.55 us
    all_to_all x2, waiting for transfers between devices, exchanged(): return lax.all_to_all(x, 'col', 0, 0, tiled=True, axis_index_groups=groups)  3.06 us
    ppermute x4, starting transfers between devices, swapped(): lax.ppermute(x, axis, [(i, i ^ 1 << bit) for i in range(lax.axis_size(axi...  2.09 us
    ppermute x4, waiting for transfers between devices, swapped(): lax.ppermute(x, axis, [(i, i ^ 1 << bit) for i in range(lax.axis_size(axi...  1.83 us
    ppermute x3, waiting for transfers between devices, per_device(): lax.ppermute(other if col_step else same, ('row', 'col'), pairs)  1.45 us
  transfers between devices with their start and end apart: 9, of which 6 were waited for; matrix products, arithmetic and copies ran while one was open for 0% of the time, Pallas kernels for 18%

profile of v2, /device:TPU:0, one launch (start us, length us, event | category | flops | bytes accessed | tf_op | source)
XLA Modules:
  0.0 35.7 jit_solution(12864136480563676225)
XLA Ops:
  0.0 2.9 %compress.1 = (bf16[1024,128]{1,0:T(8,128)(2,1)S(1)}, bf16[8,128,128]{2,1,0:T(8,128)(2,1)}, bf16[128,128]{1,0:T(8,128)(2,1)S(1)}, f32[128,128]{1,0:T(8,128)S(1)}) custom-call(s32[8]{0:T(128)} %owner_hbm.3, f32[1024,128]{1,0:T(8,128)} %x_hbm.1, bf16[1024,1024]{1,0:T(8,128)(2,1)} %compress_hbm.1, bf16[1024,256]{1,0:T(8,128)(2,1)} %root_hbm.2), custom_call_target="tpu_custom_call" | custom-call | flops 335544320 | bytes 1310720 | tf_op jit(solution)/shard_map/compress/pallas_call | solution.py:58
  2.9 0.5 %collective-permute-start = (bf16[128,128]{1,0:T(8,128)(2,1)S(1)}, bf16[128,128]{1,0:T(8,128)(2,1)S(1)}, u32[]{:S(2)}, u32[]{:S(2)}) collective-permute-start(bf16[128,128]{1,0:T(8,128)(2,1)S(1)} %get-tuple-element.27), channel_id=1, source_target_pairs={{0,8},{8,0},{16,24},{24,16},{1,9},{9,1},{17,25},{25,17},{2,10},{10... | collective-permute-start | bytes 98312 | tf_op jit(solution)/shard_map/ppermute | solution.py:21
  3.4 7.4 %all-to-all-start = ((bf16[8,128,128]{2,1,0:T(8,128)(2,1)}), bf16[8,128,128]{2,1,0:T(8,128)(2,1)S(1)}, u32[]{:S(2)}, u32[]{:S(2)}) async-start(bf16[8,128,128]{2,1,0:T(8,128)(2,1)} %get-tuple-element.25), calls=%async_computation | async-start | bytes 524288 | tf_op jit(solution)/shard_map/all_to_all | solution.py:38
  10.9 0.0 collective-permute-done.got_ref
  10.9 0.0 copy-start
  10.9 1.6 %collective-permute-start.2 = (bf16[64,128]{1,0:T(8,128)(2,1)S(1)}, bf16[64,128]{1,0:T(8,128)(2,1)S(1)}, u32[]{:S(2)}, u32[]{:S(2)}) collective-permute-start(bf16[64,128]{1,0:T(8,128)(2,1)S(1)} %get-tuple-element.33), channel_id=1, source_target_pairs={{0,16},{1,17},{2,18},{3,19},{4,20},{5,21},{6,22},{7,23},{8,24},{9,... | collective-permute-start | bytes 49160 | tf_op jit(solution)/shard_map/ppermute | solution.py:306
  12.4 1.4 %collective-permute-start.3 = (bf16[64,128]{1,0:T(8,128)(2,1)S(1)}, bf16[64,128]{1,0:T(8,128)(2,1)S(1)}, u32[]{:S(2)}, u32[]{:S(2)}) collective-permute-start(bf16[64,128]{1,0:T(8,128)(2,1)S(1)} %get-tuple-element.32), channel_id=1, source_target_pairs={{0,17},{1,16},{2,19},{3,18},{4,21},{5,20},{6,23},{7,22},{8,25},{9,... | collective-permute-start | bytes 49160 | tf_op jit(solution)/shard_map/ppermute | solution.py:306
  13.9 0.6 %collective-permute-start.1 = (bf16[64,128]{1,0:T(8,128)(2,1)S(1)}, bf16[64,128]{1,0:T(8,128)(2,1)S(1)}, u32[]{:S(2)}, u32[]{:S(2)}) collective-permute-start(bf16[64,128]{1,0:T(8,128)(2,1)S(1)} %get-tuple-element.32), channel_id=1, source_target_pairs={{0,1},{1,0},{2,3},{3,2},{4,5},{5,4},{6,7},{7,6},{8,9},{9,8},{10,11... | collective-permute-start | bytes 49160 | tf_op jit(solution)/shard_map/ppermute | solution.py:306
  14.4 1.7 %levels.1 = (f32[2,256,128]{2,1,0:T(8,128)S(1)}, bf16[2,256,128]{2,1,0:T(8,128)(2,1)S(1)}) custom-call(bf16[1024,128]{1,0:T(8,128)(2,1)S(1)} %get-tuple-element.29.low_ref, bf16[2,1024,256]{2,1,0:T(8,128)(2,1)} %basis_hbm.1), custom_call_target="tpu_custom_call" | custom-call | flops 134217728 | bytes 524288 | tf_op jit(solution)/shard_map/levels/pallas_call | solution.py:58
  16.2 0.0 collective-permute-done.2.refs_1_
  16.2 0.9 %collective-permute-done.3.refs_2_ = bf16[64,128]{1,0:T(8,128)(2,1)S(1)} collective-permute-done((bf16[64,128]{1,0:T(8,128)(2,1)S(1)}, bf16[64,128]{1,0:T(8,128)(2,1)S(1)}, u32[]{:S(2)}, u32[]{:S(2)}) %collective-permute-start.3) | collective-permute-done | bytes 16416 | tf_op jit(solution)/shard_map/ppermute | solution.py:306
  17.1 0.5 %collective-permute-done.1.refs_0_ = bf16[64,128]{1,0:T(8,128)(2,1)S(1)} collective-permute-done((bf16[64,128]{1,0:T(8,128)(2,1)S(1)}, bf16[64,128]{1,0:T(8,128)(2,1)S(1)}, u32[]{:S(2)}, u32[]{:S(2)}) %collective-permute-start.1) | collective-permute-done | bytes 16416 | tf_op jit(solution)/shard_map/ppermute | solution.py:306
  17.6 0.9 %all-to-all-done.arrived_ref = bf16[8,128,128]{2,1,0:T(8,128)(2,1)S(1)} async-done(((bf16[8,128,128]{2,1,0:T(8,128)(2,1)}), bf16[8,128,128]{2,1,0:T(8,128)(2,1)S(1)}, u32[]{:S(2)}, u32[]{:S(2)}) %all-to-all-start) | async-done | bytes 262176 | tf_op jit(solution)/shard_map/all_to_all | solution.py:38
  18.6 0.0 copy-done
  18.6 1.4 %middle.1 = (bf16[8,192,128]{2,1,0:T(8,128)(2,1)}, bf16[1024,128]{1,0:T(8,128)(2,1)S(1)}, f32[2,256,128]{2,1,0:T(8,128)S(1)}) custom-call(bf16[1024,1024]{1,0:T(8,128)(2,1)S(1)} %copy-done, bf16[8,128,128]{2,1,0:T(8,128)(2,1)S(1)} %all-to-all-done.arrived_ref, ...), custom_call_target="tpu_custom_call", output_to_operand_aliasing={{1}: (2, {}), {2}: (3, {})} | custom-call | flops 268435456 | bytes 1048576 | tf_op jit(solution)/shard_map/middle/pallas_call | solution.py:58
  20.0 4.3 %all-to-all-start.1 = ((bf16[8,192,128]{2,1,0:T(8,128)(2,1)}), bf16[8,192,128]{2,1,0:T(8,128)(2,1)S(1)}, u32[]{:S(2)}, u32[]{:S(2)}) async-start(bf16[8,192,128]{2,1,0:T(8,128)(2,1)} %get-tuple-element.34), calls=%async_computation.1 | async-start | bytes 786432 | tf_op jit(solution)/shard_map/all_to_all | solution.py:38
  24.3 0.0 collective-permute-start.4
  24.3 1.3 %collective-permute-done.4 = bf16[2,256,128]{2,1,0:T(8,128)(2,1)S(1)} collective-permute-done((bf16[2,256,128]{2,1,0:T(8,128)(2,1)S(1)}, bf16[2,256,128]{2,1,0:T(8,128)(2,1)S(1)}, u32[]{:S(2)}, u32[]{:S(2)}) %collective-permute-start.4) | collective-permute-done | bytes 131104 | tf_op jit(solution)/shard_map/ppermute | solution.py:21
  25.6 0.7 %level_sum.1 = (f32[1,256,128]{2,1,0:T(8,128)}, bf16[1,256,128]{2,1,0:T(8,128)(2,1)S(1)}) custom-call(f32[1,256,128]{2,1,0:T(8,128)S(1)} %slice.10.keep_ref, bf16[1,256,128]{2,1,0:T(8,128)(2,1)S(1)} %get-tuple-element.45.got_ref), custom_call_target="tpu_custom_call" | custom-call | tf_op jit(solution)/shard_map/level_sum/pallas_call | solution.py:58
  26.3 1.5 %collective-permute-start.5 = (bf16[1,256,128]{2,1,0:T(8,128)(2,1)S(1)}, bf16[1,256,128]{2,1,0:T(8,128)(2,1)S(1)}, u32[]{:S(2)}, u32[]{:S(2)}) collective-permute-start(bf16[1,256,128]{2,1,0:T(8,128)(2,1)S(1)} %get-tuple-element.40), channel_id=1, source_target_pairs={{0,16},{8,24},{16,0},{24,8},{1,17},{9,25},{17,1},{25,9},{2,18},{10... | collective-permute-start | bytes 196616 | tf_op jit(solution)/shard_map/ppermute | solution.py:21
  27.8 2.9 %dense.1 = (f32[1024,128]{1,0:T(8,128)S(1)}, bf16[2,1024,256]{2,1,0:T(8,128)(2,1)S(1)}, bf16[1024,1024]{1,0:T(8,128)(2,1)S(1)}, bf16[1024,256]{1,0:T(8,128)(2,1)S(1)}) custom-call(s32[8]{0:T(128)} %owner_hbm.3, bf16[1024,128]{1,0:T(8,128)(2,1)S(1)} %get-tuple-element.35.low_ref, bf16[1024,1024]{1,0:T(8,128)(2,1)} %inverse_hbm.1, ...), custom_call_target="tpu_custom_call" | custom-call | flops 268435456 | bytes 1048576 | tf_op jit(solution)/shard_map/dense/pallas_call | solution.py:58
  30.7 0.0 collective-permute-done.5
  30.8 0.4 %couple.1.partial_ref = f32[1024,128]{1,0:T(8,128)S(1)} custom-call(f32[1024,128]{1,0:T(8,128)S(1)} %get-tuple-element.36.dense_ref, bf16[2,1024,256]{2,1,0:T(8,128)(2,1)S(1)} %get-tuple-element.37.expand_ref, bf16[256,128]{1,0:T(8,128)(2,1)S(1)} %get-tuple-element.46.refs_0_, bf16[256,128]{1,0:T(8,128)(2,1)S(1)} %bitcast.3), custom_call_target="tpu_custom_call" | custom-call | flops 134217728 | bytes 524288 | tf_op jit(solution)/shard_map/couple/pallas_call | solution.py:58
  31.2 2.1 %all-to-all-done.1.returned_ref = bf16[8,192,128]{2,1,0:T(8,128)(2,1)S(1)} async-done(((bf16[8,192,128]{2,1,0:T(8,128)(2,1)}), bf16[8,192,128]{2,1,0:T(8,128)(2,1)S(1)}, u32[]{:S(2)}, u32[]{:S(2)}) %all-to-all-start.1) | async-done | bytes 393248 | tf_op jit(solution)/shard_map/all_to_all | solution.py:38
  33.3 0.1 collective-permute-start.6
  33.4 0.7 %expand.1.partial_ref = f32[1024,128]{1,0:T(8,128)S(1)} custom-call(f32[1024,128]{1,0:T(8,128)S(1)} %get-tuple-element.41.partial_ref, bf16[1024,1024]{1,0:T(8,128)(2,1)S(1)} %get-tuple-element.42.expand_ref, bf16[8,192,128]{2,1,0:T(8,128)(2,1)S(1)} %all-to-all-done.1.returned_ref), custom_call_target="tpu_custom_call" | custom-call | flops 268435456 | bytes 1048576 | tf_op jit(solution)/shard_map/expand/pallas_call | solution.py:58
  34.1 0.5 %collective-permute-done.6.other_ref = bf16[128,128]{1,0:T(8,128)(2,1)S(1)} collective-permute-done((bf16[128,128]{1,0:T(8,128)(2,1)S(1)}, bf16[128,128]{1,0:T(8,128)(2,1)S(1)}, u32[]{:S(2)}, u32[]{:S(2)}) %collective-permute-start.6) | collective-permute-done | bytes 32800 | tf_op jit(solution)/shard_map/ppermute | solution.py:21
  34.6 1.1 %final.1 = f32[1024,128]{1,0:T(8,128)} custom-call(f32[1024,128]{1,0:T(8,128)S(1)} %expand.1.partial_ref, bf16[1024,256]{1,0:T(8,128)(2,1)S(1)} %get-tuple-element.43.root_expand_ref, bf16[128,128]{1,0:T(8,128)(2,1)S(1)} %get-tuple-element.44.mine_ref, bf16[128,128]{1,0:T(8,128)(2,1)S(1)} %collective-permute-done.6.other_ref), custom_call_target="tpu_custom_call" | custom-call | flops 67108864 | bytes 262144 | tf_op jit(solution)/shard_map/final/pallas_call | solution.py:58
  (4 shorter events, 0.1 us)
Async XLA Ops:
  2.9 7.9 %collective-permute-start = (bf16[128,128]{1,0:T(8,128)(2,1)S(1)}, bf16[128,128]{1,0:T(8,128)(2,1)S(1)}, u32[]{:S(2)}, u32[]{:S(2)}) collective-permute-start(bf16[128,128]{1,0:T(8,128)(2,1)S(1)} %get-tuple-element.27), channel_id=1, source_target_pairs={{0,8},{8,0},{16,24},{24,16},{1,9},{9,1},{17,25},{25,17},{2,10},{10... | collective-permute-start | bytes 98312 | tf_op jit(solution)/shard_map/ppermute | solution.py:21
  3.4 15.1 %all-to-all-start = ((bf16[8,128,128]{2,1,0:T(8,128)(2,1)}), bf16[8,128,128]{2,1,0:T(8,128)(2,1)S(1)}, u32[]{:S(2)}, u32[]{:S(2)}) async-start(bf16[8,128,128]{2,1,0:T(8,128)(2,1)} %get-tuple-element.25), calls=%async_computation | async-start | bytes 524288 | tf_op jit(solution)/shard_map/all_to_all | solution.py:38
  10.9 7.7 %copy-start = (bf16[1024,1024]{1,0:T(8,128)(2,1)S(1)}, bf16[1024,1024]{1,0:T(8,128)(2,1)}, u32[]{:S(2)}) copy-start(bf16[1024,1024]{1,0:T(8,128)(2,1)} %middle_ref.1) | copy-start | bytes 6291460
  10.9 5.3 %collective-permute-start.2 = (bf16[64,128]{1,0:T(8,128)(2,1)S(1)}, bf16[64,128]{1,0:T(8,128)(2,1)S(1)}, u32[]{:S(2)}, u32[]{:S(2)}) collective-permute-start(bf16[64,128]{1,0:T(8,128)(2,1)S(1)} %get-tuple-element.33), channel_id=1, source_target_pairs={{0,16},{1,17},{2,18},{3,19},{4,20},{5,21},{6,22},{7,23},{8,24},{9,... | collective-permute-start | bytes 49160 | tf_op jit(solution)/shard_map/ppermute | solution.py:306
  12.4 4.6 %collective-permute-start.3 = (bf16[64,128]{1,0:T(8,128)(2,1)S(1)}, bf16[64,128]{1,0:T(8,128)(2,1)S(1)}, u32[]{:S(2)}, u32[]{:S(2)}) collective-permute-start(bf16[64,128]{1,0:T(8,128)(2,1)S(1)} %get-tuple-element.32), channel_id=1, source_target_pairs={{0,17},{1,16},{2,19},{3,18},{4,21},{5,20},{6,23},{7,22},{8,25},{9,... | collective-permute-start | bytes 49160 | tf_op jit(solution)/shard_map/ppermute | solution.py:306
  13.9 3.7 %collective-permute-start.1 = (bf16[64,128]{1,0:T(8,128)(2,1)S(1)}, bf16[64,128]{1,0:T(8,128)(2,1)S(1)}, u32[]{:S(2)}, u32[]{:S(2)}) collective-permute-start(bf16[64,128]{1,0:T(8,128)(2,1)S(1)} %get-tuple-element.32), channel_id=1, source_target_pairs={{0,1},{1,0},{2,3},{3,2},{4,5},{5,4},{6,7},{7,6},{8,9},{9,8},{10,11... | collective-permute-start | bytes 49160 | tf_op jit(solution)/shard_map/ppermute | solution.py:306
  20.0 13.3 %all-to-all-start.1 = ((bf16[8,192,128]{2,1,0:T(8,128)(2,1)}), bf16[8,192,128]{2,1,0:T(8,128)(2,1)S(1)}, u32[]{:S(2)}, u32[]{:S(2)}) async-start(bf16[8,192,128]{2,1,0:T(8,128)(2,1)} %get-tuple-element.34), calls=%async_computation.1 | async-start | bytes 786432 | tf_op jit(solution)/shard_map/all_to_all | solution.py:38
  24.3 1.3 %collective-permute-start.4 = (bf16[2,256,128]{2,1,0:T(8,128)(2,1)S(1)}, bf16[2,256,128]{2,1,0:T(8,128)(2,1)S(1)}, u32[]{:S(2)}, u32[]{:S(2)}) collective-permute-start(bf16[2,256,128]{2,1,0:T(8,128)(2,1)S(1)} %get-tuple-element.38), channel_id=1, source_target_pairs={{0,8},{8,0},{16,24},{24,16},{1,9},{9,1},{17,25},{25,17},{2,10},{10... | collective-permute-start | bytes 393224 | tf_op jit(solution)/shard_map/ppermute | solution.py:21
  26.3 4.4 %collective-permute-start.5 = (bf16[1,256,128]{2,1,0:T(8,128)(2,1)S(1)}, bf16[1,256,128]{2,1,0:T(8,128)(2,1)S(1)}, u32[]{:S(2)}, u32[]{:S(2)}) collective-permute-start(bf16[1,256,128]{2,1,0:T(8,128)(2,1)S(1)} %get-tuple-element.40), channel_id=1, source_target_pairs={{0,16},{8,24},{16,0},{24,8},{1,17},{9,25},{17,1},{25,9},{2,18},{10... | collective-permute-start | bytes 196616 | tf_op jit(solution)/shard_map/ppermute | solution.py:21
  33.3 1.3 %collective-permute-start.6 = (bf16[128,128]{1,0:T(8,128)(2,1)S(1)}, bf16[128,128]{1,0:T(8,128)(2,1)S(1)}, u32[]{:S(2)}, u32[]{:S(2)}) collective-permute-start(bf16[128,128]{1,0:T(8,128)(2,1)S(1)} %get-tuple-element.44.mine_ref), channel_id=1, source_target_pairs={{0,8},{8,0},{16,24},{24,16},{1,9},{9,1},{17,25},{25,17},{2,10},{10... | collective-permute-start | bytes 98312 | tf_op jit(solution)/shard_map/ppermute | solution.py:21

commit v3 on v2

--- a/solution.py
+++ b/solution.py
@@ -21,20 +21,24 @@
     return lax.ppermute(x, axis, [(i, i ^ 1 << bit) for i in range(lax.axis_size(axis))])
 
 
-def slots(count):
-    block = count // 4
-    return [quarter * block + i for quarter in (2, 0, 1, 3) for i in range(block)]
-
-
-def slot_of(device, count):
-    block = count // 4
-    quarter = device // block
-    moved = jnp.where(quarter == 3, 3, jnp.where(quarter == 2, 0, quarter + 1))
-    return device + (moved - quarter) * block
-
-
-def exchanged(x):
-    groups = [slots(lax.axis_size("col"))]
+out_order = (4, 2, 0, 6, 5, 3, 1, 7)
+back_order = (4, 2, 0, 6, 5, 3, 1, 7)
+
+
+def slots(order, count):
+    parts = len(order)
+    if count % parts:
+        return list(range(count))
+    block = count // parts
+    return [part * block + i for part in order for i in range(block)]
+
+
+def slot_of(order, device, count):
+    return sum(jnp.where(device == d, i, 0) for i, d in enumerate(slots(order, count)))
+
+
+def exchanged(x, order):
+    groups = [slots(order, lax.axis_size("col"))]
     return lax.all_to_all(x, "col", 0, 0, tiled=True, axis_index_groups=groups)
 
 
@@ -102,7 +106,7 @@
         out_ref[b * count : (b + 1) * count] = product.reshape(count, size, -1)
         for k in range(b * count, (b + 1) * count):
             outs.append(
-                pltpu.make_async_copy(out_ref.at[k], out_hbm.at[slot_of(owner_ref[k], pieces)], out_sems.at[k])
+                pltpu.make_async_copy(out_ref.at[k], out_hbm.at[slot_of(out_order, owner_ref[k], pieces)], out_sems.at[k])
             )
             outs[-1].start()
     root_copy.wait()
@@ -176,22 +180,24 @@
     for got_ref in got:
         total += got_ref[...].astype(f32)
     part = total.astype(bf16)
-    order = slots(pieces)
+    order = slots(out_order, pieces)
+    back = slots(back_order, pieces)
     arrived = jnp.concatenate([arrived_ref[order.index(c)] for c in range(pieces)], axis=0)
     copies = []
     for k in range(pieces):
         out_ref[k, :size] = mul(middle_ref[k * size : (k + 1) * size, :], arrived).astype(bf16)
         out_ref[k, size:] = part
-        copies.append(pltpu.make_async_copy(out_ref.at[k], out_hbm.at[order.index(k)], sems.at[k]))
+        copies.append(pltpu.make_async_copy(out_ref.at[k], out_hbm.at[back.index(k)], sems.at[k]))
         copies[-1].start()
     for copy in copies:
         copy.wait()
 
 
-def add_kernel(keep_ref, got_ref, sum_ref, send_ref):
-    total = keep_ref[...] + got_ref[...].astype(f32)
-    sum_ref[...] = total
+def add_kernel(keep_ref, got_ref, send_ref, *sum_ref):
+    total = keep_ref[1:] + got_ref[1:].astype(f32)
     send_ref[...] = total.astype(bf16)
+    if sum_ref:
+        sum_ref[0][...] = total
 
 
 def dense_kernel(
@@ -210,7 +216,7 @@
     size = expand_ref.shape[1] // pieces
     expand_copies = []
     for k in range(pieces):
-        place = pl.ds(pl.multiple_of(slot_of(owner_ref[k], pieces) * size, size), size)
+        place = pl.ds(pl.multiple_of(slot_of(back_order, owner_ref[k], pieces) * size, size), size)
         expand_copies.append(
             pltpu.make_async_copy(
                 expand_hbm.at[:, k * size : (k + 1) * size], expand_ref.at[:, place], expand_sems.at[k]
@@ -227,14 +233,14 @@
     out_ref = refs[-1]
     total = dense_ref[...]
     for level, sibling_ref in enumerate(refs[:-1]):
-        total += mul(expand_ref[level], sibling_ref[...])
+        total += mul(expand_ref[level], sibling_ref[0])
     out_ref[...] = total
 
 
 def root_kernel(returned_ref, partial_ref, out_ref, through_ref):
     part = out_ref.shape[0] // 2
     size = returned_ref.shape[1] - part
-    order = slots(returned_ref.shape[0])
+    order = slots(back_order, returned_ref.shape[0])
     for parity in range(2):
         total = jnp.zeros((part, out_ref.shape[1]), f32)
         for k in range(returned_ref.shape[0]):
@@ -279,7 +285,7 @@
 
     low, outgoing, send, keep = compressed(owner_map, right_side, compress, root_project)
     got = swapped(send, "row", 0)
-    arrived = exchanged(outgoing)
+    arrived = exchanged(outgoing, out_order)
     own, same, other, low = call(
         split_kernel,
         [
@@ -327,7 +333,7 @@
         flops=2 * middle.shape[0] * middle.shape[1] * columns,
         name="middle",
     )
-    returned = exchanged(mixed)
+    returned = exchanged(mixed, back_order)
 
     dense, row_expand, expand, root_expand = call(
         dense_kernel,
@@ -348,16 +354,14 @@
         flops=2 * rows * rows * columns,
         name="dense",
     )
-    siblings = [partner[0]]
+    siblings = [partner]
     for bit in range(1, levels):
-        running, level_send = call(
-            add_kernel,
-            [shape(running[1:].shape, f32), shape(running[1:].shape, bf16)],
-            (running[1:], partner[1:]),
-            name="level_sum",
-        )
+        dims = (levels - bit, rank, columns)
+        out = [shape(dims, bf16)] + [shape(dims, f32)] * (bit + 1 < levels)
+        level_send, *running = call(add_kernel, out, (running, partner), name="level_sum")
+        running = running[0] if running else None
         partner = swapped(level_send, "row", bit)
-        siblings.append(partner[0])
+        siblings.append(partner)
     partial = call(
         couple_kernel,
         shape((rows, columns), f32),

time: 36.1 us -> 34.5 us (0.956)
  waiting for transfers between devices: 6.34 us -> 4.17 us
  starting transfers between devices: 17.3 us -> 18.6 us
  Pallas kernels: 11.9 us -> 11.3 us
    all_to_all x2, waiting for transfers between devices: 3.06 us -> 0.89 us  [exchanged(): return lax.all_to_all(x, 'col', 0, 0, tiled=True, axis_index_groups=groups)]
    all_to_all x2, starting transfers between devices: 11.7 us -> 12.9 us  [exchanged(): return lax.all_to_all(x, 'col', 0, 0, tiled=True, axis_index_groups=groups)]
    pallas_call x10, Pallas kernels: 11.9 us -> 11.3 us  [call(): pl.pallas_call(kernel, out_shape=out, in_specs=specs or [in_vmem] * len(a...]
  transfers between devices with their start and end apart: 9 -> 9, of which waited for: 6 -> 5; matrix products, arithmetic and copies ran while one was open for 0% -> 0% of each run, Pallas kernels for 18% -> 17%
where the time goes in v3:
time: 34.5 us; the launch traced here: 34.1 us
  starting transfers between devices  18.6 us (54%)
  Pallas kernels  11.3 us (33%)
  waiting for transfers between devices  4.17 us (12%)
    all_to_all x2, starting transfers between devices, exchanged(): return lax.all_to_all(x, 'col', 0, 0, tiled=True, axis_index_groups=groups)  12.9 us
    pallas_call x10, Pallas kernels, call(): pl.pallas_call(kernel, out_shape=out, in_specs=specs or [in_vmem] * len(a...  11.3 us
    ppermute x3, starting transfers between devices, per_device(): lax.ppermute(other if col_step else same, ('row', 'col'), pairs)  3.55 us
    ppermute x4, starting transfers between devices, swapped(): lax.ppermute(x, axis, [(i, i ^ 1 << bit) for i in range(lax.axis_size(axi...  2.15 us
    ppermute x4, waiting for transfers between devices, swapped(): lax.ppermute(x, axis, [(i, i ^ 1 << bit) for i in range(lax.axis_size(axi...  1.83 us
    ppermute x3, waiting for transfers between devices, per_device(): lax.ppermute(other if col_step else same, ('row', 'col'), pairs)  1.45 us
    all_to_all x2, waiting for transfers between devices, exchanged(): return lax.all_to_all(x, 'col', 0, 0, tiled=True, axis_index_groups=groups)  0.89 us
  transfers between devices with their start and end apart: 9, of which 5 were waited for; matrix products, arithmetic and copies ran while one was open for 0% of the time, Pallas kernels for 17%

profile of v3, /device:TPU:0, one launch (start us, length us, event | category | flops | bytes accessed | tf_op | source)
XLA Modules:
  0.0 34.1 jit_solution(4060950539375727104)
XLA Ops:
  0.0 2.9 %compress.1 = (bf16[1024,128]{1,0:T(8,128)(2,1)S(1)}, bf16[8,128,128]{2,1,0:T(8,128)(2,1)}, bf16[128,128]{1,0:T(8,128)(2,1)S(1)}, f32[128,128]{1,0:T(8,128)S(1)}) custom-call(s32[8]{0:T(128)} %owner_hbm.3, f32[1024,128]{1,0:T(8,128)} %x_hbm.1, bf16[1024,1024]{1,0:T(8,128)(2,1)} %compress_hbm.1, bf16[1024,256]{1,0:T(8,128)(2,1)} %root_hbm.2), custom_call_target="tpu_custom_call" | custom-call | flops 335544320 | bytes 1310720 | tf_op jit(solution)/shard_map/compress/pallas_call | solution.py:62
  2.9 0.5 %collective-permute-start = (bf16[128,128]{1,0:T(8,128)(2,1)S(1)}, bf16[128,128]{1,0:T(8,128)(2,1)S(1)}, u32[]{:S(2)}, u32[]{:S(2)}) collective-permute-start(bf16[128,128]{1,0:T(8,128)(2,1)S(1)} %get-tuple-element.26), channel_id=1, source_target_pairs={{0,8},{8,0},{16,24},{24,16},{1,9},{9,1},{17,25},{25,17},{2,10},{10... | collective-permute-start | bytes 98312 | tf_op jit(solution)/shard_map/ppermute | solution.py:21
  3.4 7.4 %all-to-all-start = ((bf16[8,128,128]{2,1,0:T(8,128)(2,1)}), bf16[8,128,128]{2,1,0:T(8,128)(2,1)S(1)}, u32[]{:S(2)}, u32[]{:S(2)}) async-start(bf16[8,128,128]{2,1,0:T(8,128)(2,1)} %get-tuple-element.24), calls=%async_computation | async-start | bytes 524288 | tf_op jit(solution)/shard_map/all_to_all | solution.py:42
  10.9 0.0 collective-permute-done.got_ref
  10.9 0.0 copy-start
  10.9 1.6 %collective-permute-start.2 = (bf16[64,128]{1,0:T(8,128)(2,1)S(1)}, bf16[64,128]{1,0:T(8,128)(2,1)S(1)}, u32[]{:S(2)}, u32[]{:S(2)}) collective-permute-start(bf16[64,128]{1,0:T(8,128)(2,1)S(1)} %get-tuple-element.32), channel_id=1, source_target_pairs={{0,16},{1,17},{2,18},{3,19},{4,20},{5,21},{6,22},{7,23},{8,24},{9,... | collective-permute-start | bytes 49160 | tf_op jit(solution)/shard_map/ppermute | solution.py:312
  12.4 1.4 %collective-permute-start.3 = (bf16[64,128]{1,0:T(8,128)(2,1)S(1)}, bf16[64,128]{1,0:T(8,128)(2,1)S(1)}, u32[]{:S(2)}, u32[]{:S(2)}) collective-permute-start(bf16[64,128]{1,0:T(8,128)(2,1)S(1)} %get-tuple-element.31), channel_id=1, source_target_pairs={{0,17},{1,16},{2,19},{3,18},{4,21},{5,20},{6,23},{7,22},{8,25},{9,... | collective-permute-start | bytes 49160 | tf_op jit(solution)/shard_map/ppermute | solution.py:312
  13.9 0.6 %collective-permute-start.1 = (bf16[64,128]{1,0:T(8,128)(2,1)S(1)}, bf16[64,128]{1,0:T(8,128)(2,1)S(1)}, u32[]{:S(2)}, u32[]{:S(2)}) collective-permute-start(bf16[64,128]{1,0:T(8,128)(2,1)S(1)} %get-tuple-element.31), channel_id=1, source_target_pairs={{0,1},{1,0},{2,3},{3,2},{4,5},{5,4},{6,7},{7,6},{8,9},{9,8},{10,11... | collective-permute-start | bytes 49160 | tf_op jit(solution)/shard_map/ppermute | solution.py:312
  14.4 1.7 %levels.1 = (f32[2,256,128]{2,1,0:T(8,128)S(1)}, bf16[2,256,128]{2,1,0:T(8,128)(2,1)S(1)}) custom-call(bf16[1024,128]{1,0:T(8,128)(2,1)S(1)} %get-tuple-element.28.low_ref, bf16[2,1024,256]{2,1,0:T(8,128)(2,1)} %basis_hbm.1), custom_call_target="tpu_custom_call" | custom-call | flops 134217728 | bytes 524288 | tf_op jit(solution)/shard_map/levels/pallas_call | solution.py:62
  16.2 0.0 collective-permute-done.2.refs_1_
  16.2 1.0 %collective-permute-done.3.refs_2_ = bf16[64,128]{1,0:T(8,128)(2,1)S(1)} collective-permute-done((bf16[64,128]{1,0:T(8,128)(2,1)S(1)}, bf16[64,128]{1,0:T(8,128)(2,1)S(1)}, u32[]{:S(2)}, u32[]{:S(2)}) %collective-permute-start.3) | collective-permute-done | bytes 16416 | tf_op jit(solution)/shard_map/ppermute | solution.py:312
  17.1 0.5 %collective-permute-done.1.refs_0_ = bf16[64,128]{1,0:T(8,128)(2,1)S(1)} collective-permute-done((bf16[64,128]{1,0:T(8,128)(2,1)S(1)}, bf16[64,128]{1,0:T(8,128)(2,1)S(1)}, u32[]{:S(2)}, u32[]{:S(2)}) %collective-permute-start.1) | collective-permute-done | bytes 16416 | tf_op jit(solution)/shard_map/ppermute | solution.py:312
  17.6 0.0 all-to-all-done.arrived_ref
  17.6 0.0 copy-done
  17.6 1.4 %middle.1 = (bf16[8,192,128]{2,1,0:T(8,128)(2,1)}, bf16[1024,128]{1,0:T(8,128)(2,1)S(1)}, f32[2,256,128]{2,1,0:T(8,128)S(1)}) custom-call(bf16[1024,1024]{1,0:T(8,128)(2,1)S(1)} %copy-done, bf16[8,128,128]{2,1,0:T(8,128)(2,1)S(1)} %all-to-all-done.arrived_ref, ...), custom_call_target="tpu_custom_call", output_to_operand_aliasing={{1}: (2, {}), {2}: (3, {})} | custom-call | flops 268435456 | bytes 1048576 | tf_op jit(solution)/shard_map/middle/pallas_call | solution.py:62
  19.0 5.5 %all-to-all-start.1 = ((bf16[8,192,128]{2,1,0:T(8,128)(2,1)}), bf16[8,192,128]{2,1,0:T(8,128)(2,1)S(1)}, u32[]{:S(2)}, u32[]{:S(2)}) async-start(bf16[8,192,128]{2,1,0:T(8,128)(2,1)} %get-tuple-element.33), calls=%async_computation.1 | async-start | bytes 786432 | tf_op jit(solution)/shard_map/all_to_all | solution.py:42
  24.5 0.0 collective-permute-start.4
  24.5 1.3 %collective-permute-done.4.got_ref.refs_0_ = bf16[2,256,128]{2,1,0:T(8,128)(2,1)S(1)} collective-permute-done((bf16[2,256,128]{2,1,0:T(8,128)(2,1)S(1)}, bf16[2,256,128]{2,1,0:T(8,128)(2,1)S(1)}, u32[]{:S(2)}, u32[]{:S(2)}) %collective-permute-start.4) | collective-permute-done | bytes 131104 | tf_op jit(solution)/shard_map/ppermute | solution.py:21
  25.9 1.6 %collective-permute-start.5 = (bf16[1,256,128]{2,1,0:T(8,128)(2,1)S(1)}, bf16[1,256,128]{2,1,0:T(8,128)(2,1)S(1)}, u32[]{:S(2)}, u32[]{:S(2)}) collective-permute-start(bf16[1,256,128]{2,1,0:T(8,128)(2,1)S(1)} %level_sum.1), channel_id=1, source_target_pairs={{0,16},{8,24},{16,0},{24,8},{1,17},{9,25},{17,1},{25,9},{2,18},{10... | collective-permute-start | bytes 196616 | tf_op jit(solution)/shard_map/ppermute | solution.py:21
  27.5 2.9 %dense.1 = (f32[1024,128]{1,0:T(8,128)S(1)}, bf16[2,1024,256]{2,1,0:T(8,128)(2,1)S(1)}, bf16[1024,1024]{1,0:T(8,128)(2,1)S(1)}, bf16[1024,256]{1,0:T(8,128)(2,1)S(1)}) custom-call(s32[8]{0:T(128)} %owner_hbm.3, bf16[1024,128]{1,0:T(8,128)(2,1)S(1)} %get-tuple-element.34.low_ref, bf16[1024,1024]{1,0:T(8,128)(2,1)} %inverse_hbm.1, ...), custom_call_target="tpu_custom_call" | custom-call | flops 268435456 | bytes 1048576 | tf_op jit(solution)/shard_map/dense/pallas_call | solution.py:62
  30.4 0.0 collective-permute-done.5.refs_1_
  30.4 0.4 %couple.1.partial_ref = f32[1024,128]{1,0:T(8,128)S(1)} custom-call(f32[1024,128]{1,0:T(8,128)S(1)} %get-tuple-element.35.dense_ref, bf16[2,1024,256]{2,1,0:T(8,128)(2,1)S(1)} %get-tuple-element.36.expand_ref, bf16[2,256,128]{2,1,0:T(8,128)(2,1)S(1)} %collective-permute-done.4.got_ref.refs_0_, bf16[1,256,128]{2,1,0:T(8,128)(2,1)S(1)} %collective-permute-done.5.refs_1_), custom_call_target="tpu_custom_call" | custom-call | flops 134217728 | bytes 524288 | tf_op jit(solution)/shard_map/couple/pallas_call | solution.py:62
  30.8 0.9 %all-to-all-done.1.returned_ref = bf16[8,192,128]{2,1,0:T(8,128)(2,1)S(1)} async-done(((bf16[8,192,128]{2,1,0:T(8,128)(2,1)}), bf16[8,192,128]{2,1,0:T(8,128)(2,1)S(1)}, u32[]{:S(2)}, u32[]{:S(2)}) %all-to-all-start.1) | async-done | bytes 393248 | tf_op jit(solution)/shard_map/all_to_all | solution.py:42
  31.8 0.1 collective-permute-start.6
  31.8 0.7 %expand.1.partial_ref = f32[1024,128]{1,0:T(8,128)S(1)} custom-call(f32[1024,128]{1,0:T(8,128)S(1)} %get-tuple-element.39.partial_ref, bf16[1024,1024]{1,0:T(8,128)(2,1)S(1)} %get-tuple-element.40.expand_ref, bf16[8,192,128]{2,1,0:T(8,128)(2,1)S(1)} %all-to-all-done.1.returned_ref), custom_call_target="tpu_custom_call" | custom-call | flops 268435456 | bytes 1048576 | tf_op jit(solution)/shard_map/expand/pallas_call | solution.py:62
  32.5 0.5 %collective-permute-done.6.other_ref = bf16[128,128]{1,0:T(8,128)(2,1)S(1)} collective-permute-done((bf16[128,128]{1,0:T(8,128)(2,1)S(1)}, bf16[128,128]{1,0:T(8,128)(2,1)S(1)}, u32[]{:S(2)}, u32[]{:S(2)}) %collective-permute-start.6) | collective-permute-done | bytes 32800 | tf_op jit(solution)/shard_map/ppermute | solution.py:21
  33.0 1.1 %final.1 = f32[1024,128]{1,0:T(8,128)} custom-call(f32[1024,128]{1,0:T(8,128)S(1)} %expand.1.partial_ref, bf16[1024,256]{1,0:T(8,128)(2,1)S(1)} %get-tuple-element.41.root_expand_ref, bf16[128,128]{1,0:T(8,128)(2,1)S(1)} %get-tuple-element.42.mine_ref, bf16[128,128]{1,0:T(8,128)(2,1)S(1)} %collective-permute-done.6.other_ref), custom_call_target="tpu_custom_call" | custom-call | flops 67108864 | bytes 262144 | tf_op jit(solution)/shard_map/final/pallas_call | solution.py:62
  (3 shorter events, 0.1 us)
Async XLA Ops:
  2.9 7.9 %collective-permute-start = (bf16[128,128]{1,0:T(8,128)(2,1)S(1)}, bf16[128,128]{1,0:T(8,128)(2,1)S(1)}, u32[]{:S(2)}, u32[]{:S(2)}) collective-permute-start(bf16[128,128]{1,0:T(8,128)(2,1)S(1)} %get-tuple-element.26), channel_id=1, source_target_pairs={{0,8},{8,0},{16,24},{24,16},{1,9},{9,1},{17,25},{25,17},{2,10},{10... | collective-permute-start | bytes 98312 | tf_op jit(solution)/shard_map/ppermute | solution.py:21
  3.4 14.2 %all-to-all-start = ((bf16[8,128,128]{2,1,0:T(8,128)(2,1)}), bf16[8,128,128]{2,1,0:T(8,128)(2,1)S(1)}, u32[]{:S(2)}, u32[]{:S(2)}) async-start(bf16[8,128,128]{2,1,0:T(8,128)(2,1)} %get-tuple-element.24), calls=%async_computation | async-start | bytes 524288 | tf_op jit(solution)/shard_map/all_to_all | solution.py:42
  10.9 6.8 %copy-start = (bf16[1024,1024]{1,0:T(8,128)(2,1)S(1)}, bf16[1024,1024]{1,0:T(8,128)(2,1)}, u32[]{:S(2)}) copy-start(bf16[1024,1024]{1,0:T(8,128)(2,1)} %middle_ref.1) | copy-start | bytes 6291460
  10.9 5.3 %collective-permute-start.2 = (bf16[64,128]{1,0:T(8,128)(2,1)S(1)}, bf16[64,128]{1,0:T(8,128)(2,1)S(1)}, u32[]{:S(2)}, u32[]{:S(2)}) collective-permute-start(bf16[64,128]{1,0:T(8,128)(2,1)S(1)} %get-tuple-element.32), channel_id=1, source_target_pairs={{0,16},{1,17},{2,18},{3,19},{4,20},{5,21},{6,22},{7,23},{8,24},{9,... | collective-permute-start | bytes 49160 | tf_op jit(solution)/shard_map/ppermute | solution.py:312
  12.4 4.7 %collective-permute-start.3 = (bf16[64,128]{1,0:T(8,128)(2,1)S(1)}, bf16[64,128]{1,0:T(8,128)(2,1)S(1)}, u32[]{:S(2)}, u32[]{:S(2)}) collective-permute-start(bf16[64,128]{1,0:T(8,128)(2,1)S(1)} %get-tuple-element.31), channel_id=1, source_target_pairs={{0,17},{1,16},{2,19},{3,18},{4,21},{5,20},{6,23},{7,22},{8,25},{9,... | collective-permute-start | bytes 49160 | tf_op jit(solution)/shard_map/ppermute | solution.py:312
  13.9 3.7 %collective-permute-start.1 = (bf16[64,128]{1,0:T(8,128)(2,1)S(1)}, bf16[64,128]{1,0:T(8,128)(2,1)S(1)}, u32[]{:S(2)}, u32[]{:S(2)}) collective-permute-start(bf16[64,128]{1,0:T(8,128)(2,1)S(1)} %get-tuple-element.31), channel_id=1, source_target_pairs={{0,1},{1,0},{2,3},{3,2},{4,5},{5,4},{6,7},{7,6},{8,9},{9,8},{10,11... | collective-permute-start | bytes 49160 | tf_op jit(solution)/shard_map/ppermute | solution.py:312
  19.0 12.7 %all-to-all-start.1 = ((bf16[8,192,128]{2,1,0:T(8,128)(2,1)}), bf16[8,192,128]{2,1,0:T(8,128)(2,1)S(1)}, u32[]{:S(2)}, u32[]{:S(2)}) async-start(bf16[8,192,128]{2,1,0:T(8,128)(2,1)} %get-tuple-element.33), calls=%async_computation.1 | async-start | bytes 786432 | tf_op jit(solution)/shard_map/all_to_all | solution.py:42
  24.5 1.3 %collective-permute-start.4 = (bf16[2,256,128]{2,1,0:T(8,128)(2,1)S(1)}, bf16[2,256,128]{2,1,0:T(8,128)(2,1)S(1)}, u32[]{:S(2)}, u32[]{:S(2)}) collective-permute-start(bf16[2,256,128]{2,1,0:T(8,128)(2,1)S(1)} %get-tuple-element.37), channel_id=1, source_target_pairs={{0,8},{8,0},{16,24},{24,16},{1,9},{9,1},{17,25},{25,17},{2,10},{10... | collective-permute-start | bytes 393224 | tf_op jit(solution)/shard_map/ppermute | solution.py:21
  25.9 4.5 %collective-permute-start.5 = (bf16[1,256,128]{2,1,0:T(8,128)(2,1)S(1)}, bf16[1,256,128]{2,1,0:T(8,128)(2,1)S(1)}, u32[]{:S(2)}, u32[]{:S(2)}) collective-permute-start(bf16[1,256,128]{2,1,0:T(8,128)(2,1)S(1)} %level_sum.1), channel_id=1, source_target_pairs={{0,16},{8,24},{16,0},{24,8},{1,17},{9,25},{17,1},{25,9},{2,18},{10... | collective-permute-start | bytes 196616 | tf_op jit(solution)/shard_map/ppermute | solution.py:21
  31.8 1.3 %collective-permute-start.6 = (bf16[128,128]{1,0:T(8,128)(2,1)S(1)}, bf16[128,128]{1,0:T(8,128)(2,1)S(1)}, u32[]{:S(2)}, u32[]{:S(2)}) collective-permute-start(bf16[128,128]{1,0:T(8,128)(2,1)S(1)} %get-tuple-element.42.mine_ref), channel_id=1, source_target_pairs={{0,8},{8,0},{16,24},{24,16},{1,9},{9,1},{17,25},{25,17},{2,10},{10... | collective-permute-start | bytes 98312 | tf_op jit(solution)/shard_map/ppermute | solution.py:21

commit v4 on v3

--- a/solution.py
+++ b/solution.py
@@ -21,8 +21,8 @@
     return lax.ppermute(x, axis, [(i, i ^ 1 << bit) for i in range(lax.axis_size(axis))])
 
 
-out_order = (4, 2, 0, 6, 5, 3, 1, 7)
-back_order = (4, 2, 0, 6, 5, 3, 1, 7)
+out_order = (4, 2, 0, 7, 5, 3, 1, 6)
+back_order = (4, 2, 0, 7, 5, 3, 1, 6)
 
 
 def slots(order, count):
@@ -114,7 +114,7 @@
     half = keep_ref.shape[0]
     mine = lax.rem(lax.axis_index("row"), 2)
     keep_ref[...] = product_ref[pl.ds(pl.multiple_of(mine * half, half), half), :]
-    send_ref[...] = product_ref[pl.ds(pl.multiple_of((1 - mine) * half, half), half), :].astype(bf16)
+    send_ref[...] = product_ref[pl.ds(pl.multiple_of((1 - mine) * half, half), half), :]
     for copy in outs:
         copy.wait()
 
@@ -130,7 +130,7 @@
         [
             shape((rows, columns), bf16),
             shape(outgoing, bf16),
-            shape((rank // 2, columns), bf16),
+            shape((rank // 2, columns), f32),
             shape((rank // 2, columns), f32),
         ],
         (left(owner_map), left(x), left(compress), left(root_project)),
@@ -249,19 +249,26 @@
         out_ref[parity * part : (parity + 1) * part] = total.astype(bf16)
 
 
-def expand_kernel(partial_ref, expand_ref, returned_ref, out_ref):
+def half_of(root_expand_ref, rows, which):
+    half = rows.shape[0]
+    return mul(root_expand_ref[:, pl.ds(pl.multiple_of(which * half, half), half)], rows)
+
+
+def expand_kernel(partial_ref, expand_ref, returned_ref, root_expand_ref, mine_ref, out_ref):
     pieces = returned_ref.shape[0]
     size = expand_ref.shape[1] // pieces
     returned = jnp.concatenate([returned_ref[k, :size] for k in range(pieces)], axis=0)
-    out_ref[...] = partial_ref[...] + mul(expand_ref[...], returned)
-
-
-def final_kernel(partial_ref, root_expand_ref, mine_ref, other_ref, out_ref, root_ref):
-    half = mine_ref.shape[0]
     mine = lax.rem(lax.axis_index("row"), 2)
-    root_ref[pl.ds(pl.multiple_of(mine * half, half), half), :] = mine_ref[...]
-    root_ref[pl.ds(pl.multiple_of((1 - mine) * half, half), half), :] = other_ref[...]
-    out_ref[...] = partial_ref[...] + mul(root_expand_ref[...], root_ref[...])
+    out_ref[...] = (
+        partial_ref[...]
+        + mul(expand_ref[...], returned)
+        + half_of(root_expand_ref, mine_ref[...], mine)
+    )
+
+
+def final_kernel(partial_ref, root_expand_ref, other_ref, out_ref):
+    mine = lax.rem(lax.axis_index("row"), 2)
+    out_ref[...] = partial_ref[...] + half_of(root_expand_ref, other_ref[...], 1 - mine)
 
 
 def per_device(
@@ -381,15 +388,14 @@
     partial = call(
         expand_kernel,
         shape((rows, columns), f32),
-        (partial, expand, returned),
+        (partial, expand, returned, root_expand, root_mine),
         flops=2 * rows * expand.shape[1] * columns,
         name="expand",
     )
     return call(
         final_kernel,
         shape((rows, columns), f32),
-        (partial, root_expand, root_mine, root_other),
-        scratch=[pltpu.VMEM((rank, columns), bf16)],
+        (partial, root_expand, root_other),
         flops=2 * rows * rank * columns,
         name="final",
     )

time: 34.5 us -> 34.1 us (0.988)
  waiting for transfers between devices: 4.17 us -> 3.8 us
where the time goes in v4:
time: 34.1 us; the launch traced here: 33.7 us
  starting transfers between devices  18.6 us (55%)
  Pallas kernels  11.2 us (33%)
  waiting for transfers between devices  3.8 us (11%)
    all_to_all x2, starting transfers between devices, exchanged(): return lax.all_to_all(x, 'col', 0, 0, tiled=True, axis_index_groups=groups)  12.9 us
    pallas_call x10, Pallas kernels, call(): pl.pallas_call(kernel, out_shape=out, in_specs=specs or [in_vmem] * len(a...  11.2 us
    ppermute x3, starting transfers between devices, per_device(): lax.ppermute(other if col_step else same, ('row', 'col'), pairs)  3.55 us
    ppermute x4, starting transfers between devices, swapped(): lax.ppermute(x, axis, [(i, i ^ 1 << bit) for i in range(lax.axis_size(axi...  2.15 us
    ppermute x4, waiting for transfers between devices, swapped(): lax.ppermute(x, axis, [(i, i ^ 1 << bit) for i in range(lax.axis_size(axi...  1.76 us
    ppermute x3, waiting for transfers between devices, per_device(): lax.ppermute(other if col_step else same, ('row', 'col'), pairs)  1.45 us
  transfers between devices with their start and end apart: 9, of which 5 were waited for; matrix products, arithmetic and copies ran while one was open for 0% of the time, Pallas kernels for 17%

profile of v4, /device:TPU:0, one launch (start us, length us, event | category | flops | bytes accessed | tf_op | source)
XLA Modules:
  0.0 33.7 jit_solution(3311402940161336233)
XLA Ops:
  0.0 2.9 %compress.1 = (bf16[1024,128]{1,0:T(8,128)(2,1)S(1)}, bf16[8,128,128]{2,1,0:T(8,128)(2,1)}, f32[128,128]{1,0:T(8,128)S(1)}, f32[128,128]{1,0:T(8,128)S(1)}) custom-call(s32[8]{0:T(128)} %owner_hbm.3, f32[1024,128]{1,0:T(8,128)} %x_hbm.1, bf16[1024,1024]{1,0:T(8,128)(2,1)} %compress_hbm.1, bf16[1024,256]{1,0:T(8,128)(2,1)} %root_hbm.2), custom_call_target="tpu_custom_call" | custom-call | flops 335544320 | bytes 1310720 | tf_op jit(solution)/shard_map/compress/pallas_call | solution.py:62
  2.9 0.5 %collective-permute-start = (f32[128,128]{1,0:T(8,128)S(1)}, f32[128,128]{1,0:T(8,128)S(1)}, u32[]{:S(2)}, u32[]{:S(2)}) collective-permute-start(f32[128,128]{1,0:T(8,128)S(1)} %get-tuple-element.26), channel_id=1, source_target_pairs={{0,8},{8,0},{16,24},{24,16},{1,9},{9,1},{17,25},{25,17},{2,10},{10... | collective-permute-start | bytes 196616 | tf_op jit(solution)/shard_map/ppermute | solution.py:21
  3.4 7.4 %all-to-all-start = ((bf16[8,128,128]{2,1,0:T(8,128)(2,1)}), bf16[8,128,128]{2,1,0:T(8,128)(2,1)S(1)}, u32[]{:S(2)}, u32[]{:S(2)}) async-start(bf16[8,128,128]{2,1,0:T(8,128)(2,1)} %get-tuple-element.24), calls=%async_computation | async-start | bytes 524288 | tf_op jit(solution)/shard_map/all_to_all | solution.py:42
  10.9 0.0 collective-permute-done.got_ref
  10.9 0.0 copy-start
  10.9 1.6 %collective-permute-start.2 = (bf16[64,128]{1,0:T(8,128)(2,1)S(1)}, bf16[64,128]{1,0:T(8,128)(2,1)S(1)}, u32[]{:S(2)}, u32[]{:S(2)}) collective-permute-start(bf16[64,128]{1,0:T(8,128)(2,1)S(1)} %get-tuple-element.32), channel_id=1, source_target_pairs={{0,16},{1,17},{2,18},{3,19},{4,20},{5,21},{6,22},{7,23},{8,24},{9,... | collective-permute-start | bytes 49160 | tf_op jit(solution)/shard_map/ppermute | solution.py:319
  12.4 1.4 %collective-permute-start.3 = (bf16[64,128]{1,0:T(8,128)(2,1)S(1)}, bf16[64,128]{1,0:T(8,128)(2,1)S(1)}, u32[]{:S(2)}, u32[]{:S(2)}) collective-permute-start(bf16[64,128]{1,0:T(8,128)(2,1)S(1)} %get-tuple-element.31), channel_id=1, source_target_pairs={{0,17},{1,16},{2,19},{3,18},{4,21},{5,20},{6,23},{7,22},{8,25},{9,... | collective-permute-start | bytes 49160 | tf_op jit(solution)/shard_map/ppermute | solution.py:319
  13.9 0.6 %collective-permute-start.1 = (bf16[64,128]{1,0:T(8,128)(2,1)S(1)}, bf16[64,128]{1,0:T(8,128)(2,1)S(1)}, u32[]{:S(2)}, u32[]{:S(2)}) collective-permute-start(bf16[64,128]{1,0:T(8,128)(2,1)S(1)} %get-tuple-element.31), channel_id=1, source_target_pairs={{0,1},{1,0},{2,3},{3,2},{4,5},{5,4},{6,7},{7,6},{8,9},{9,8},{10,11... | collective-permute-start | bytes 49160 | tf_op jit(solution)/shard_map/ppermute | solution.py:319
  14.4 1.7 %levels.1 = (f32[2,256,128]{2,1,0:T(8,128)S(1)}, bf16[2,256,128]{2,1,0:T(8,128)(2,1)S(1)}) custom-call(bf16[1024,128]{1,0:T(8,128)(2,1)S(1)} %get-tuple-element.28.low_ref, bf16[2,1024,256]{2,1,0:T(8,128)(2,1)} %basis_hbm.1), custom_call_target="tpu_custom_call" | custom-call | flops 134217728 | bytes 524288 | tf_op jit(solution)/shard_map/levels/pallas_call | solution.py:62
  16.2 0.0 collective-permute-done.2.refs_1_
  16.2 1.0 %collective-permute-done.3.refs_2_ = bf16[64,128]{1,0:T(8,128)(2,1)S(1)} collective-permute-done((bf16[64,128]{1,0:T(8,128)(2,1)S(1)}, bf16[64,128]{1,0:T(8,128)(2,1)S(1)}, u32[]{:S(2)}, u32[]{:S(2)}) %collective-permute-start.3) | collective-permute-done | bytes 16416 | tf_op jit(solution)/shard_map/ppermute | solution.py:319
  17.1 0.5 %collective-permute-done.1.refs_0_ = bf16[64,128]{1,0:T(8,128)(2,1)S(1)} collective-permute-done((bf16[64,128]{1,0:T(8,128)(2,1)S(1)}, bf16[64,128]{1,0:T(8,128)(2,1)S(1)}, u32[]{:S(2)}, u32[]{:S(2)}) %collective-permute-start.1) | collective-permute-done | bytes 16416 | tf_op jit(solution)/shard_map/ppermute | solution.py:319
  17.6 0.0 all-to-all-done.arrived_ref
  17.6 0.0 copy-done
  17.6 1.4 %middle.1 = (bf16[8,192,128]{2,1,0:T(8,128)(2,1)}, bf16[1024,128]{1,0:T(8,128)(2,1)S(1)}, f32[2,256,128]{2,1,0:T(8,128)S(1)}) custom-call(bf16[1024,1024]{1,0:T(8,128)(2,1)S(1)} %copy-done, bf16[8,128,128]{2,1,0:T(8,128)(2,1)S(1)} %all-to-all-done.arrived_ref, ...), custom_call_target="tpu_custom_call", output_to_operand_aliasing={{1}: (2, {}), {2}: (3, {})} | custom-call | flops 268435456 | bytes 1048576 | tf_op jit(solution)/shard_map/middle/pallas_call | solution.py:62
  19.0 5.5 %all-to-all-start.1 = ((bf16[8,192,128]{2,1,0:T(8,128)(2,1)}), bf16[8,192,128]{2,1,0:T(8,128)(2,1)S(1)}, u32[]{:S(2)}, u32[]{:S(2)}) async-start(bf16[8,192,128]{2,1,0:T(8,128)(2,1)} %get-tuple-element.33), calls=%async_computation.1 | async-start | bytes 786432 | tf_op jit(solution)/shard_map/all_to_all | solution.py:42
  24.5 0.0 collective-permute-start.4
  24.5 1.3 %collective-permute-done.4.got_ref.refs_0_ = bf16[2,256,128]{2,1,0:T(8,128)(2,1)S(1)} collective-permute-done((bf16[2,256,128]{2,1,0:T(8,128)(2,1)S(1)}, bf16[2,256,128]{2,1,0:T(8,128)(2,1)S(1)}, u32[]{:S(2)}, u32[]{:S(2)}) %collective-permute-start.4) | collective-permute-done | bytes 131104 | tf_op jit(solution)/shard_map/ppermute | solution.py:21
  25.9 1.6 %collective-permute-start.5 = (bf16[1,256,128]{2,1,0:T(8,128)(2,1)S(1)}, bf16[1,256,128]{2,1,0:T(8,128)(2,1)S(1)}, u32[]{:S(2)}, u32[]{:S(2)}) collective-permute-start(bf16[1,256,128]{2,1,0:T(8,128)(2,1)S(1)} %level_sum.1), channel_id=1, source_target_pairs={{0,16},{8,24},{16,0},{24,8},{1,17},{9,25},{17,1},{25,9},{2,18},{10... | collective-permute-start | bytes 196616 | tf_op jit(solution)/shard_map/ppermute | solution.py:21
  27.5 2.9 %dense.1 = (f32[1024,128]{1,0:T(8,128)S(1)}, bf16[2,1024,256]{2,1,0:T(8,128)(2,1)S(1)}, bf16[1024,1024]{1,0:T(8,128)(2,1)S(1)}, bf16[1024,256]{1,0:T(8,128)(2,1)S(1)}) custom-call(s32[8]{0:T(128)} %owner_hbm.3, bf16[1024,128]{1,0:T(8,128)(2,1)S(1)} %get-tuple-element.34.low_ref, bf16[1024,1024]{1,0:T(8,128)(2,1)} %inverse_hbm.1, ...), custom_call_target="tpu_custom_call" | custom-call | flops 268435456 | bytes 1048576 | tf_op jit(solution)/shard_map/dense/pallas_call | solution.py:62
  30.4 0.0 collective-permute-done.5.refs_1_
  30.4 0.4 %couple.1.partial_ref = f32[1024,128]{1,0:T(8,128)S(1)} custom-call(f32[1024,128]{1,0:T(8,128)S(1)} %get-tuple-element.35.dense_ref, bf16[2,1024,256]{2,1,0:T(8,128)(2,1)S(1)} %get-tuple-element.36.expand_ref, bf16[2,256,128]{2,1,0:T(8,128)(2,1)S(1)} %collective-permute-done.4.got_ref.refs_0_, bf16[1,256,128]{2,1,0:T(8,128)(2,1)S(1)} %collective-permute-done.5.refs_1_), custom_call_target="tpu_custom_call" | custom-call | flops 134217728 | bytes 524288 | tf_op jit(solution)/shard_map/couple/pallas_call | solution.py:62
  30.8 0.6 %all-to-all-done.1.returned_ref = bf16[8,192,128]{2,1,0:T(8,128)(2,1)S(1)} async-done(((bf16[8,192,128]{2,1,0:T(8,128)(2,1)}), bf16[8,192,128]{2,1,0:T(8,128)(2,1)S(1)}, u32[]{:S(2)}, u32[]{:S(2)}) %all-to-all-start.1) | async-done | bytes 393248 | tf_op jit(solution)/shard_map/all_to_all | solution.py:42
  31.5 0.1 collective-permute-start.6
  31.5 0.8 %expand.1.partial_ref = f32[1024,128]{1,0:T(8,128)S(1)} custom-call(f32[1024,128]{1,0:T(8,128)S(1)} %get-tuple-element.39.partial_ref, bf16[1024,1024]{1,0:T(8,128)(2,1)S(1)} %get-tuple-element.40.expand_ref, bf16[8,192,128]{2,1,0:T(8,128)(2,1)S(1)} %all-to-all-done.1.returned_ref, bf16[1024,256]{1,0:T(8,128)(2,1)S(1)} %get-tuple-element.41.root_expand_ref, ...), custom_call_target="tpu_custom_call" | custom-call | flops 268435456 | bytes 1048576 | tf_op jit(solution)/shard_map/expand/pallas_call | solution.py:62
  32.3 0.4 %collective-permute-done.6.other_ref = bf16[128,128]{1,0:T(8,128)(2,1)S(1)} collective-permute-done((bf16[128,128]{1,0:T(8,128)(2,1)S(1)}, bf16[128,128]{1,0:T(8,128)(2,1)S(1)}, u32[]{:S(2)}, u32[]{:S(2)}) %collective-permute-start.6) | collective-permute-done | bytes 32800 | tf_op jit(solution)/shard_map/ppermute | solution.py:21
  32.7 1.0 %final.1 = f32[1024,128]{1,0:T(8,128)} custom-call(f32[1024,128]{1,0:T(8,128)S(1)} %expand.1.partial_ref, bf16[1024,256]{1,0:T(8,128)(2,1)S(1)} %get-tuple-element.41.root_expand_ref, bf16[128,128]{1,0:T(8,128)(2,1)S(1)} %collective-permute-done.6.other_ref), custom_call_target="tpu_custom_call" | custom-call | flops 67108864 | bytes 262144 | tf_op jit(solution)/shard_map/final/pallas_call | solution.py:62
  (3 shorter events, 0.1 us)
Async XLA Ops:
  2.9 7.9 %collective-permute-start = (f32[128,128]{1,0:T(8,128)S(1)}, f32[128,128]{1,0:T(8,128)S(1)}, u32[]{:S(2)}, u32[]{:S(2)}) collective-permute-start(f32[128,128]{1,0:T(8,128)S(1)} %get-tuple-element.26), channel_id=1, source_target_pairs={{0,8},{8,0},{16,24},{24,16},{1,9},{9,1},{17,25},{25,17},{2,10},{10... | collective-permute-start | bytes 196616 | tf_op jit(solution)/shard_map/ppermute | solution.py:21
  3.4 14.2 %all-to-all-start = ((bf16[8,128,128]{2,1,0:T(8,128)(2,1)}), bf16[8,128,128]{2,1,0:T(8,128)(2,1)S(1)}, u32[]{:S(2)}, u32[]{:S(2)}) async-start(bf16[8,128,128]{2,1,0:T(8,128)(2,1)} %get-tuple-element.24), calls=%async_computation | async-start | bytes 524288 | tf_op jit(solution)/shard_map/all_to_all | solution.py:42
  10.9 6.8 %copy-start = (bf16[1024,1024]{1,0:T(8,128)(2,1)S(1)}, bf16[1024,1024]{1,0:T(8,128)(2,1)}, u32[]{:S(2)}) copy-start(bf16[1024,1024]{1,0:T(8,128)(2,1)} %middle_ref.1) | copy-start | bytes 6291460
  10.9 5.3 %collective-permute-start.2 = (bf16[64,128]{1,0:T(8,128)(2,1)S(1)}, bf16[64,128]{1,0:T(8,128)(2,1)S(1)}, u32[]{:S(2)}, u32[]{:S(2)}) collective-permute-start(bf16[64,128]{1,0:T(8,128)(2,1)S(1)} %get-tuple-element.32), channel_id=1, source_target_pairs={{0,16},{1,17},{2,18},{3,19},{4,20},{5,21},{6,22},{7,23},{8,24},{9,... | collective-permute-start | bytes 49160 | tf_op jit(solution)/shard_map/ppermute | solution.py:319
  12.4 4.7 %collective-permute-start.3 = (bf16[64,128]{1,0:T(8,128)(2,1)S(1)}, bf16[64,128]{1,0:T(8,128)(2,1)S(1)}, u32[]{:S(2)}, u32[]{:S(2)}) collective-permute-start(bf16[64,128]{1,0:T(8,128)(2,1)S(1)} %get-tuple-element.31), channel_id=1, source_target_pairs={{0,17},{1,16},{2,19},{3,18},{4,21},{5,20},{6,23},{7,22},{8,25},{9,... | collective-permute-start | bytes 49160 | tf_op jit(solution)/shard_map/ppermute | solution.py:319
  13.9 3.7 %collective-permute-start.1 = (bf16[64,128]{1,0:T(8,128)(2,1)S(1)}, bf16[64,128]{1,0:T(8,128)(2,1)S(1)}, u32[]{:S(2)}, u32[]{:S(2)}) collective-permute-start(bf16[64,128]{1,0:T(8,128)(2,1)S(1)} %get-tuple-element.31), channel_id=1, source_target_pairs={{0,1},{1,0},{2,3},{3,2},{4,5},{5,4},{6,7},{7,6},{8,9},{9,8},{10,11... | collective-permute-start | bytes 49160 | tf_op jit(solution)/shard_map/ppermute | solution.py:319
  19.0 12.4 %all-to-all-start.1 = ((bf16[8,192,128]{2,1,0:T(8,128)(2,1)}), bf16[8,192,128]{2,1,0:T(8,128)(2,1)S(1)}, u32[]{:S(2)}, u32[]{:S(2)}) async-start(bf16[8,192,128]{2,1,0:T(8,128)(2,1)} %get-tuple-element.33), calls=%async_computation.1 | async-start | bytes 786432 | tf_op jit(solution)/shard_map/all_to_all | solution.py:42
  24.5 1.3 %collective-permute-start.4 = (bf16[2,256,128]{2,1,0:T(8,128)(2,1)S(1)}, bf16[2,256,128]{2,1,0:T(8,128)(2,1)S(1)}, u32[]{:S(2)}, u32[]{:S(2)}) collective-permute-start(bf16[2,256,128]{2,1,0:T(8,128)(2,1)S(1)} %get-tuple-element.37), channel_id=1, source_target_pairs={{0,8},{8,0},{16,24},{24,16},{1,9},{9,1},{17,25},{25,17},{2,10},{10... | collective-permute-start | bytes 393224 | tf_op jit(solution)/shard_map/ppermute | solution.py:21
  25.9 4.5 %collective-permute-start.5 = (bf16[1,256,128]{2,1,0:T(8,128)(2,1)S(1)}, bf16[1,256,128]{2,1,0:T(8,128)(2,1)S(1)}, u32[]{:S(2)}, u32[]{:S(2)}) collective-permute-start(bf16[1,256,128]{2,1,0:T(8,128)(2,1)S(1)} %level_sum.1), channel_id=1, source_target_pairs={{0,16},{8,24},{16,0},{24,8},{1,17},{9,25},{17,1},{25,9},{2,18},{10... | collective-permute-start | bytes 196616 | tf_op jit(solution)/shard_map/ppermute | solution.py:21
  31.5 1.3 %collective-permute-start.6 = (bf16[128,128]{1,0:T(8,128)(2,1)S(1)}, bf16[128,128]{1,0:T(8,128)(2,1)S(1)}, u32[]{:S(2)}, u32[]{:S(2)}) collective-permute-start(bf16[128,128]{1,0:T(8,128)(2,1)S(1)} %get-tuple-element.42.mine_ref), channel_id=1, source_target_pairs={{0,8},{8,0},{16,24},{24,16},{1,9},{9,1},{17,25},{25,17},{2,10},{10... | collective-permute-start | bytes 98312 | tf_op jit(solution)/shard_map/ppermute | solution.py:21

commit v5 on v4

--- a/solution.py
+++ b/solution.py
@@ -184,11 +184,13 @@
     back = slots(back_order, pieces)
     arrived = jnp.concatenate([arrived_ref[order.index(c)] for c in range(pieces)], axis=0)
     copies = []
-    for k in range(pieces):
-        out_ref[k, :size] = mul(middle_ref[k * size : (k + 1) * size, :], arrived).astype(bf16)
-        out_ref[k, size:] = part
-        copies.append(pltpu.make_async_copy(out_ref.at[k], out_hbm.at[back.index(k)], sems.at[k]))
-        copies[-1].start()
+    for first in range(0, pieces, 2):
+        product = mul(middle_ref[first * size : (first + 2) * size, :], arrived).astype(bf16)
+        for k in range(first, first + 2):
+            out_ref[k, :size] = product[(k - first) * size : (k - first + 1) * size]
+            out_ref[k, size:] = part
+            copies.append(pltpu.make_async_copy(out_ref.at[k], out_hbm.at[back.index(k)], sems.at[k]))
+            copies[-1].start()
     for copy in copies:
         copy.wait()
 
@@ -201,16 +203,14 @@
 
 
 def dense_kernel(
-    owner_hbm, low_ref, inverse_hbm, row_hbm, expand_hbm, root_hbm,
-    out_ref, row_ref, expand_ref, root_ref,
+    owner_hbm, low_ref, inverse_hbm, expand_hbm,
+    out_ref, expand_ref,
     owner_ref, inverse_ref, sems, expand_sems,
 ):
     owner_copy = pltpu.make_async_copy(owner_hbm, owner_ref, sems.at[0])
     inverse_copy = pltpu.make_async_copy(inverse_hbm, inverse_ref, sems.at[1])
-    row_copy = pltpu.make_async_copy(row_hbm, row_ref, sems.at[2])
-    root_copy = pltpu.make_async_copy(root_hbm, root_ref, sems.at[3])
-    for copy in (owner_copy, inverse_copy, row_copy, root_copy):
-        copy.start()
+    owner_copy.start()
+    inverse_copy.start()
     owner_copy.wait()
     pieces = expand_sems.shape[0]
     size = expand_ref.shape[1] // pieces
@@ -225,7 +225,7 @@
         expand_copies[-1].start()
     inverse_copy.wait()
     out_ref[...] = mul(inverse_ref[...], low_ref[...])
-    for copy in (row_copy, root_copy, *expand_copies):
+    for copy in expand_copies:
         copy.wait()
 
 
@@ -342,20 +342,18 @@
     )
     returned = exchanged(mixed, back_order)
 
-    dense, row_expand, expand, root_expand = call(
+    dense, expand = call(
         dense_kernel,
         [
             shape((rows, columns), f32),
-            pltpu.VMEM(row_expand.shape, bf16),
             pltpu.VMEM(expand.shape, bf16),
-            pltpu.VMEM(root_expand.shape, bf16),
         ],
-        (left(owner_map), low, left(leaf_inverse), left(row_expand), left(expand), left(root_expand)),
-        specs=[in_place, in_vmem] + [in_place] * 4,
+        (left(owner_map), low, left(leaf_inverse), left(expand)),
+        specs=[in_place, in_vmem] + [in_place] * 2,
         scratch=[
             pltpu.SMEM(owner_map.shape, jnp.int32),
             pltpu.VMEM(leaf_inverse.shape, bf16),
-            pltpu.SemaphoreType.DMA((4,)),
+            pltpu.SemaphoreType.DMA((2,)),
             pltpu.SemaphoreType.DMA((col_count,)),
         ],
         flops=2 * rows * rows * columns,
@@ -372,7 +370,7 @@
     partial = call(
         couple_kernel,
         shape((rows, columns), f32),
-        (dense, row_expand, *siblings),
+        (dense, ahead(row_expand), *siblings),
         flops=2 * rows * rank * levels * columns,
         name="couple",
     )
@@ -388,14 +386,14 @@
     partial = call(
         expand_kernel,
         shape((rows, columns), f32),
-        (partial, expand, returned, root_expand, root_mine),
+        (partial, expand, returned, ahead(root_expand), root_mine),
         flops=2 * rows * expand.shape[1] * columns,
         name="expand",
     )
     return call(
         final_kernel,
         shape((rows, columns), f32),
-        (partial, root_expand, root_other),
+        (partial, ahead(root_expand), root_other),
         flops=2 * rows * rank * columns,
         name="final",
     )

time: 34.1 us -> 34.1 us (level)
  transfers between devices with their start and end apart: 9 -> 9, of which waited for: 5 -> 6; matrix products, arithmetic and copies ran while one was open for 0% -> 0% of each run, Pallas kernels for 17% -> 17%
where the time goes in v5:
time: 34.1 us; the launch traced here: 33.7 us
  starting transfers between devices  18.6 us (55%)
  Pallas kernels  10.9 us (32%)
  waiting for transfers between devices  4.11 us (12%)
    all_to_all x2, starting transfers between devices, exchanged(): return lax.all_to_all(x, 'col', 0, 0, tiled=True, axis_index_groups=groups)  12.9 us
    pallas_call x10, Pallas kernels, call(): pl.pallas_call(kernel, out_shape=out, in_specs=specs or [in_vmem] * len(a...  10.9 us
    ppermute x3, starting transfers between devices, per_device(): lax.ppermute(other if col_step else same, ('row', 'col'), pairs)  3.55 us
    ppermute x4, starting transfers between devices, swapped(): lax.ppermute(x, axis, [(i, i ^ 1 << bit) for i in range(lax.axis_size(axi...  2.15 us
    ppermute x4, waiting for transfers between devices, swapped(): lax.ppermute(x, axis, [(i, i ^ 1 << bit) for i in range(lax.axis_size(axi...  1.89 us
    ppermute x3, waiting for transfers between devices, per_device(): lax.ppermute(other if col_step else same, ('row', 'col'), pairs)  1.45 us
    all_to_all x2, waiting for transfers between devices, exchanged(): return lax.all_to_all(x, 'col', 0, 0, tiled=True, axis_index_groups=groups)  0.77 us
  transfers between devices with their start and end apart: 9, of which 6 were waited for; matrix products, arithmetic and copies ran while one was open for 0% of the time, Pallas kernels for 17%

profile of v5, /device:TPU:0, one launch (start us, length us, event | category | flops | bytes accessed | tf_op | source)
XLA Modules:
  0.0 33.7 jit_solution(6623429698024550284)
XLA Ops:
  0.0 2.9 %compress.1 = (bf16[1024,128]{1,0:T(8,128)(2,1)S(1)}, bf16[8,128,128]{2,1,0:T(8,128)(2,1)}, f32[128,128]{1,0:T(8,128)S(1)}, f32[128,128]{1,0:T(8,128)S(1)}) custom-call(s32[8]{0:T(128)} %owner_hbm.3, f32[1024,128]{1,0:T(8,128)} %x_hbm.1, bf16[1024,1024]{1,0:T(8,128)(2,1)} %compress_hbm.1, bf16[1024,256]{1,0:T(8,128)(2,1)} %root_hbm.1), custom_call_target="tpu_custom_call" | custom-call | flops 335544320 | bytes 1310720 | tf_op jit(solution)/shard_map/compress/pallas_call | solution.py:62
  2.9 0.5 %collective-permute-start = (f32[128,128]{1,0:T(8,128)S(1)}, f32[128,128]{1,0:T(8,128)S(1)}, u32[]{:S(2)}, u32[]{:S(2)}) collective-permute-start(f32[128,128]{1,0:T(8,128)S(1)} %get-tuple-element.24), channel_id=1, source_target_pairs={{0,8},{8,0},{16,24},{24,16},{1,9},{9,1},{17,25},{25,17},{2,10},{10... | collective-permute-start | bytes 196616 | tf_op jit(solution)/shard_map/ppermute | solution.py:21
  3.4 7.4 %all-to-all-start = ((bf16[8,128,128]{2,1,0:T(8,128)(2,1)}), bf16[8,128,128]{2,1,0:T(8,128)(2,1)S(1)}, u32[]{:S(2)}, u32[]{:S(2)}) async-start(bf16[8,128,128]{2,1,0:T(8,128)(2,1)} %get-tuple-element.22), calls=%async_computation | async-start | bytes 524288 | tf_op jit(solution)/shard_map/all_to_all | solution.py:42
  10.9 0.0 collective-permute-done.got_ref
  10.9 0.0 copy-start
  10.9 1.6 %collective-permute-start.2 = (bf16[64,128]{1,0:T(8,128)(2,1)S(1)}, bf16[64,128]{1,0:T(8,128)(2,1)S(1)}, u32[]{:S(2)}, u32[]{:S(2)}) collective-permute-start(bf16[64,128]{1,0:T(8,128)(2,1)S(1)} %get-tuple-element.30), channel_id=1, source_target_pairs={{0,16},{1,17},{2,18},{3,19},{4,20},{5,21},{6,22},{7,23},{8,24},{9,... | collective-permute-start | bytes 49160 | tf_op jit(solution)/shard_map/ppermute | solution.py:319
  12.4 1.4 %collective-permute-start.3 = (bf16[64,128]{1,0:T(8,128)(2,1)S(1)}, bf16[64,128]{1,0:T(8,128)(2,1)S(1)}, u32[]{:S(2)}, u32[]{:S(2)}) collective-permute-start(bf16[64,128]{1,0:T(8,128)(2,1)S(1)} %get-tuple-element.29), channel_id=1, source_target_pairs={{0,17},{1,16},{2,19},{3,18},{4,21},{5,20},{6,23},{7,22},{8,25},{9,... | collective-permute-start | bytes 49160 | tf_op jit(solution)/shard_map/ppermute | solution.py:319
  13.9 0.6 %collective-permute-start.1 = (bf16[64,128]{1,0:T(8,128)(2,1)S(1)}, bf16[64,128]{1,0:T(8,128)(2,1)S(1)}, u32[]{:S(2)}, u32[]{:S(2)}) collective-permute-start(bf16[64,128]{1,0:T(8,128)(2,1)S(1)} %get-tuple-element.29), channel_id=1, source_target_pairs={{0,1},{1,0},{2,3},{3,2},{4,5},{5,4},{6,7},{7,6},{8,9},{9,8},{10,11... | collective-permute-start | bytes 49160 | tf_op jit(solution)/shard_map/ppermute | solution.py:319
  14.4 1.7 %levels.1 = (f32[2,256,128]{2,1,0:T(8,128)S(1)}, bf16[2,256,128]{2,1,0:T(8,128)(2,1)S(1)}) custom-call(bf16[1024,128]{1,0:T(8,128)(2,1)S(1)} %get-tuple-element.26.low_ref, bf16[2,1024,256]{2,1,0:T(8,128)(2,1)} %basis_hbm.1), custom_call_target="tpu_custom_call" | custom-call | flops 134217728 | bytes 524288 | tf_op jit(solution)/shard_map/levels/pallas_call | solution.py:62
  16.2 0.0 collective-permute-done.2.refs_1_
  16.2 1.0 %collective-permute-done.3.refs_2_ = bf16[64,128]{1,0:T(8,128)(2,1)S(1)} collective-permute-done((bf16[64,128]{1,0:T(8,128)(2,1)S(1)}, bf16[64,128]{1,0:T(8,128)(2,1)S(1)}, u32[]{:S(2)}, u32[]{:S(2)}) %collective-permute-start.3) | collective-permute-done | bytes 16416 | tf_op jit(solution)/shard_map/ppermute | solution.py:319
  17.1 0.5 %collective-permute-done.1.refs_0_ = bf16[64,128]{1,0:T(8,128)(2,1)S(1)} collective-permute-done((bf16[64,128]{1,0:T(8,128)(2,1)S(1)}, bf16[64,128]{1,0:T(8,128)(2,1)S(1)}, u32[]{:S(2)}, u32[]{:S(2)}) %collective-permute-start.1) | collective-permute-done | bytes 16416 | tf_op jit(solution)/shard_map/ppermute | solution.py:319
  17.6 0.0 all-to-all-done.arrived_ref
  17.6 0.0 copy-done
  17.6 1.4 %middle.1 = (bf16[8,192,128]{2,1,0:T(8,128)(2,1)}, bf16[1024,128]{1,0:T(8,128)(2,1)S(1)}, f32[2,256,128]{2,1,0:T(8,128)S(1)}) custom-call(bf16[1024,1024]{1,0:T(8,128)(2,1)S(1)} %copy-done, bf16[8,128,128]{2,1,0:T(8,128)(2,1)S(1)} %all-to-all-done.arrived_ref, ...), custom_call_target="tpu_custom_call", output_to_operand_aliasing={{1}: (2, {}), {2}: (3, {})} | custom-call | flops 268435456 | bytes 1048576 | tf_op jit(solution)/shard_map/middle/pallas_call | solution.py:62
  19.0 5.5 %all-to-all-start.1 = ((bf16[8,192,128]{2,1,0:T(8,128)(2,1)}), bf16[8,192,128]{2,1,0:T(8,128)(2,1)S(1)}, u32[]{:S(2)}, u32[]{:S(2)}) async-start(bf16[8,192,128]{2,1,0:T(8,128)(2,1)} %get-tuple-element.31), calls=%async_computation.1 | async-start | bytes 786432 | tf_op jit(solution)/shard_map/all_to_all | solution.py:42
  24.5 0.0 collective-permute-start.4
  24.5 1.3 %collective-permute-done.4.got_ref.refs_0_ = bf16[2,256,128]{2,1,0:T(8,128)(2,1)S(1)} collective-permute-done((bf16[2,256,128]{2,1,0:T(8,128)(2,1)S(1)}, bf16[2,256,128]{2,1,0:T(8,128)(2,1)S(1)}, u32[]{:S(2)}, u32[]{:S(2)}) %collective-permute-start.4) | collective-permute-done | bytes 131104 | tf_op jit(solution)/shard_map/ppermute | solution.py:21
  25.9 1.6 %collective-permute-start.5 = (bf16[1,256,128]{2,1,0:T(8,128)(2,1)S(1)}, bf16[1,256,128]{2,1,0:T(8,128)(2,1)S(1)}, u32[]{:S(2)}, u32[]{:S(2)}) collective-permute-start(bf16[1,256,128]{2,1,0:T(8,128)(2,1)S(1)} %level_sum.1), channel_id=1, source_target_pairs={{0,16},{8,24},{16,0},{24,8},{1,17},{9,25},{17,1},{25,9},{2,18},{10... | collective-permute-start | bytes 196616 | tf_op jit(solution)/shard_map/ppermute | solution.py:21
  27.5 0.0 copy-start.2
  27.5 2.6 %dense.1 = (f32[1024,128]{1,0:T(8,128)S(1)}, bf16[1024,1024]{1,0:T(8,128)(2,1)S(1)}) custom-call(s32[8]{0:T(128)} %owner_hbm.3, bf16[1024,128]{1,0:T(8,128)(2,1)S(1)} %get-tuple-element.32.low_ref, bf16[1024,1024]{1,0:T(8,128)(2,1)} %inverse_hbm.1, bf16[1024,1024]{1,0:T(8,128)(2,1)} %expand_hbm.1), custom_call_target="tpu_custom_call" | custom-call | flops 268435456 | bytes 1048576 | tf_op jit(solution)/shard_map/dense/pallas_call | solution.py:62
  30.1 0.0 copy-start.1
  30.1 0.1 collective-permute-done.5.refs_1_
  30.2 0.0 copy-done.2
  30.2 0.4 %couple.1.partial_ref = f32[1024,128]{1,0:T(8,128)S(1)} custom-call(f32[1024,128]{1,0:T(8,128)S(1)} %get-tuple-element.33.dense_ref, bf16[2,1024,256]{2,1,0:T(8,128)(2,1)S(1)} %copy-done.2, bf16[2,256,128]{2,1,0:T(8,128)(2,1)S(1)} %collective-permute-done.4.got_ref.refs_0_, bf16[1,256,128]{2,1,0:T(8,128)(2,1)S(1)} %collective-permute-done.5.refs_1_), custom_call_target="tpu_custom_call" | custom-call | flops 134217728 | bytes 524288 | tf_op jit(solution)/shard_map/couple/pallas_call | solution.py:62
  30.7 0.8 %all-to-all-done.1.returned_ref = bf16[8,192,128]{2,1,0:T(8,128)(2,1)S(1)} async-done(((bf16[8,192,128]{2,1,0:T(8,128)(2,1)}), bf16[8,192,128]{2,1,0:T(8,128)(2,1)S(1)}, u32[]{:S(2)}, u32[]{:S(2)}) %all-to-all-start.1) | async-done | bytes 393248 | tf_op jit(solution)/shard_map/all_to_all | solution.py:42
  31.5 0.1 collective-permute-start.6
  31.5 0.0 copy-done.1
  31.5 0.8 %expand.1.partial_ref = f32[1024,128]{1,0:T(8,128)S(1)} custom-call(f32[1024,128]{1,0:T(8,128)S(1)} %get-tuple-element.36.partial_ref, bf16[1024,1024]{1,0:T(8,128)(2,1)S(1)} %get-tuple-element.37.expand_ref, bf16[8,192,128]{2,1,0:T(8,128)(2,1)S(1)} %all-to-all-done.1.returned_ref, bf16[1024,256]{1,0:T(8,128)(2,1)S(1)} %copy-done.1, ...), custom_call_target="tpu_custom_call" | custom-call | flops 268435456 | bytes 1048576 | tf_op jit(solution)/shard_map/expand/pallas_call | solution.py:62
  32.3 0.4 %collective-permute-done.6.other_ref = bf16[128,128]{1,0:T(8,128)(2,1)S(1)} collective-permute-done((bf16[128,128]{1,0:T(8,128)(2,1)S(1)}, bf16[128,128]{1,0:T(8,128)(2,1)S(1)}, u32[]{:S(2)}, u32[]{:S(2)}) %collective-permute-start.6) | collective-permute-done | bytes 32800 | tf_op jit(solution)/shard_map/ppermute | solution.py:21
  32.7 1.0 %final.1 = f32[1024,128]{1,0:T(8,128)} custom-call(f32[1024,128]{1,0:T(8,128)S(1)} %expand.1.partial_ref, bf16[1024,256]{1,0:T(8,128)(2,1)S(1)} %copy-done.1, bf16[128,128]{1,0:T(8,128)(2,1)S(1)} %collective-permute-done.6.other_ref), custom_call_target="tpu_custom_call" | custom-call | flops 67108864 | bytes 262144 | tf_op jit(solution)/shard_map/final/pallas_call | solution.py:62
  (3 shorter events, 0.1 us)
Async XLA Ops:
  2.9 7.9 %collective-permute-start = (f32[128,128]{1,0:T(8,128)S(1)}, f32[128,128]{1,0:T(8,128)S(1)}, u32[]{:S(2)}, u32[]{:S(2)}) collective-permute-start(f32[128,128]{1,0:T(8,128)S(1)} %get-tuple-element.24), channel_id=1, source_target_pairs={{0,8},{8,0},{16,24},{24,16},{1,9},{9,1},{17,25},{25,17},{2,10},{10... | collective-permute-start | bytes 196616 | tf_op jit(solution)/shard_map/ppermute | solution.py:21
  3.4 14.2 %all-to-all-start = ((bf16[8,128,128]{2,1,0:T(8,128)(2,1)}), bf16[8,128,128]{2,1,0:T(8,128)(2,1)S(1)}, u32[]{:S(2)}, u32[]{:S(2)}) async-start(bf16[8,128,128]{2,1,0:T(8,128)(2,1)} %get-tuple-element.22), calls=%async_computation | async-start | bytes 524288 | tf_op jit(solution)/shard_map/all_to_all | solution.py:42
  10.9 6.8 %copy-start = (bf16[1024,1024]{1,0:T(8,128)(2,1)S(1)}, bf16[1024,1024]{1,0:T(8,128)(2,1)}, u32[]{:S(2)}) copy-start(bf16[1024,1024]{1,0:T(8,128)(2,1)} %middle_ref.1) | copy-start | bytes 6291460
  10.9 5.3 %collective-permute-start.2 = (bf16[64,128]{1,0:T(8,128)(2,1)S(1)}, bf16[64,128]{1,0:T(8,128)(2,1)S(1)}, u32[]{:S(2)}, u32[]{:S(2)}) collective-permute-start(bf16[64,128]{1,0:T(8,128)(2,1)S(1)} %get-tuple-element.30), channel_id=1, source_target_pairs={{0,16},{1,17},{2,18},{3,19},{4,20},{5,21},{6,22},{7,23},{8,24},{9,... | collective-permute-start | bytes 49160 | tf_op jit(solution)/shard_map/ppermute | solution.py:319
  12.4 4.7 %collective-permute-start.3 = (bf16[64,128]{1,0:T(8,128)(2,1)S(1)}, bf16[64,128]{1,0:T(8,128)(2,1)S(1)}, u32[]{:S(2)}, u32[]{:S(2)}) collective-permute-start(bf16[64,128]{1,0:T(8,128)(2,1)S(1)} %get-tuple-element.29), channel_id=1, source_target_pairs={{0,17},{1,16},{2,19},{3,18},{4,21},{5,20},{6,23},{7,22},{8,25},{9,... | collective-permute-start | bytes 49160 | tf_op jit(solution)/shard_map/ppermute | solution.py:319
  13.9 3.7 %collective-permute-start.1 = (bf16[64,128]{1,0:T(8,128)(2,1)S(1)}, bf16[64,128]{1,0:T(8,128)(2,1)S(1)}, u32[]{:S(2)}, u32[]{:S(2)}) collective-permute-start(bf16[64,128]{1,0:T(8,128)(2,1)S(1)} %get-tuple-element.29), channel_id=1, source_target_pairs={{0,1},{1,0},{2,3},{3,2},{4,5},{5,4},{6,7},{7,6},{8,9},{9,8},{10,11... | collective-permute-start | bytes 49160 | tf_op jit(solution)/shard_map/ppermute | solution.py:319
  19.0 12.4 %all-to-all-start.1 = ((bf16[8,192,128]{2,1,0:T(8,128)(2,1)}), bf16[8,192,128]{2,1,0:T(8,128)(2,1)S(1)}, u32[]{:S(2)}, u32[]{:S(2)}) async-start(bf16[8,192,128]{2,1,0:T(8,128)(2,1)} %get-tuple-element.31), calls=%async_computation.1 | async-start | bytes 786432 | tf_op jit(solution)/shard_map/all_to_all | solution.py:42
  24.5 1.3 %collective-permute-start.4 = (bf16[2,256,128]{2,1,0:T(8,128)(2,1)S(1)}, bf16[2,256,128]{2,1,0:T(8,128)(2,1)S(1)}, u32[]{:S(2)}, u32[]{:S(2)}) collective-permute-start(bf16[2,256,128]{2,1,0:T(8,128)(2,1)S(1)} %get-tuple-element.34), channel_id=1, source_target_pairs={{0,8},{8,0},{16,24},{24,16},{1,9},{9,1},{17,25},{25,17},{2,10},{10... | collective-permute-start | bytes 393224 | tf_op jit(solution)/shard_map/ppermute | solution.py:21
  25.9 4.3 %collective-permute-start.5 = (bf16[1,256,128]{2,1,0:T(8,128)(2,1)S(1)}, bf16[1,256,128]{2,1,0:T(8,128)(2,1)S(1)}, u32[]{:S(2)}, u32[]{:S(2)}) collective-permute-start(bf16[1,256,128]{2,1,0:T(8,128)(2,1)S(1)} %level_sum.1), channel_id=1, source_target_pairs={{0,16},{8,24},{16,0},{24,8},{1,17},{9,25},{17,1},{25,9},{2,18},{10... | collective-permute-start | bytes 196616 | tf_op jit(solution)/shard_map/ppermute | solution.py:21
  27.5 2.8 %copy-start.2 = (bf16[2,1024,256]{2,1,0:T(8,128)(2,1)S(1)}, bf16[2,1024,256]{2,1,0:T(8,128)(2,1)}, u32[]{:S(2)}) copy-start(bf16[2,1024,256]{2,1,0:T(8,128)(2,1)} %expand_ref.1) | copy-start | bytes 3145732
  30.1 1.5 %copy-start.1 = (bf16[1024,256]{1,0:T(8,128)(2,1)S(1)}, bf16[1024,256]{1,0:T(8,128)(2,1)}, u32[]{:S(2)}) copy-start(bf16[1024,256]{1,0:T(8,128)(2,1)} %root_expand_ref.3) | copy-start | bytes 1572868
  31.5 1.3 %collective-permute-start.6 = (bf16[128,128]{1,0:T(8,128)(2,1)S(1)}, bf16[128,128]{1,0:T(8,128)(2,1)S(1)}, u32[]{:S(2)}, u32[]{:S(2)}) collective-permute-start(bf16[128,128]{1,0:T(8,128)(2,1)S(1)} %get-tuple-element.38.mine_ref), channel_id=1, source_target_pairs={{0,8},{8,0},{16,24},{24,16},{1,9},{9,1},{17,25},{25,17},{2,10},{10... | collective-permute-start | bytes 98312 | tf_op jit(solution)/shard_map/ppermute | solution.py:21

commit v6 on v4

--- a/solution.py
+++ b/solution.py
@@ -184,11 +184,13 @@
     back = slots(back_order, pieces)
     arrived = jnp.concatenate([arrived_ref[order.index(c)] for c in range(pieces)], axis=0)
     copies = []
-    for k in range(pieces):
-        out_ref[k, :size] = mul(middle_ref[k * size : (k + 1) * size, :], arrived).astype(bf16)
-        out_ref[k, size:] = part
-        copies.append(pltpu.make_async_copy(out_ref.at[k], out_hbm.at[back.index(k)], sems.at[k]))
-        copies[-1].start()
+    for first in range(0, pieces, 2):
+        product = mul(middle_ref[first * size : (first + 2) * size, :], arrived).astype(bf16)
+        for k in range(first, first + 2):
+            out_ref[k, :size] = product[(k - first) * size : (k - first + 1) * size]
+            out_ref[k, size:] = part
+            copies.append(pltpu.make_async_copy(out_ref.at[k], out_hbm.at[back.index(k)], sems.at[k]))
+            copies[-1].start()
     for copy in copies:
         copy.wait()
 

time: 34.1 us -> 34.1 us (level)
  no operation moved by 1% of the time
where the time goes in v6:
time: 34.1 us; the launch traced here: 33.7 us
  starting transfers between devices  18.6 us (55%)
  Pallas kernels  11.2 us (33%)
  waiting for transfers between devices  3.8 us (11%)
    all_to_all x2, starting transfers between devices, exchanged(): return lax.all_to_all(x, 'col', 0, 0, tiled=True, axis_index_groups=groups)  12.9 us
    pallas_call x10, Pallas kernels, call(): pl.pallas_call(kernel, out_shape=out, in_specs=specs or [in_vmem] * len(a...  11.2 us
    ppermute x3, starting transfers between devices, per_device(): lax.ppermute(other if col_step else same, ('row', 'col'), pairs)  3.55 us
    ppermute x4, starting transfers between devices, swapped(): lax.ppermute(x, axis, [(i, i ^ 1 << bit) for i in range(lax.axis_size(axi...  2.15 us
    ppermute x4, waiting for transfers between devices, swapped(): lax.ppermute(x, axis, [(i, i ^ 1 << bit) for i in range(lax.axis_size(axi...  1.76 us
    ppermute x3, waiting for transfers between devices, per_device(): lax.ppermute(other if col_step else same, ('row', 'col'), pairs)  1.45 us
  transfers between devices with their start and end apart: 9, of which 5 were waited for; matrix products, arithmetic and copies ran while one was open for 0% of the time, Pallas kernels for 17%

profile of v6, /device:TPU:0, one launch (start us, length us, event | category | flops | bytes accessed | tf_op | source)
XLA Modules:
  0.0 33.7 jit_solution(11656633888145004661)
XLA Ops:
  0.0 2.9 %compress.1 = (bf16[1024,128]{1,0:T(8,128)(2,1)S(1)}, bf16[8,128,128]{2,1,0:T(8,128)(2,1)}, f32[128,128]{1,0:T(8,128)S(1)}, f32[128,128]{1,0:T(8,128)S(1)}) custom-call(s32[8]{0:T(128)} %owner_hbm.3, f32[1024,128]{1,0:T(8,128)} %x_hbm.1, bf16[1024,1024]{1,0:T(8,128)(2,1)} %compress_hbm.1, bf16[1024,256]{1,0:T(8,128)(2,1)} %root_hbm.2), custom_call_target="tpu_custom_call" | custom-call | flops 335544320 | bytes 1310720 | tf_op jit(solution)/shard_map/compress/pallas_call | solution.py:62
  2.9 0.5 %collective-permute-start = (f32[128,128]{1,0:T(8,128)S(1)}, f32[128,128]{1,0:T(8,128)S(1)}, u32[]{:S(2)}, u32[]{:S(2)}) collective-permute-start(f32[128,128]{1,0:T(8,128)S(1)} %get-tuple-element.26), channel_id=1, source_target_pairs={{0,8},{8,0},{16,24},{24,16},{1,9},{9,1},{17,25},{25,17},{2,10},{10... | collective-permute-start | bytes 196616 | tf_op jit(solution)/shard_map/ppermute | solution.py:21
  3.4 7.4 %all-to-all-start = ((bf16[8,128,128]{2,1,0:T(8,128)(2,1)}), bf16[8,128,128]{2,1,0:T(8,128)(2,1)S(1)}, u32[]{:S(2)}, u32[]{:S(2)}) async-start(bf16[8,128,128]{2,1,0:T(8,128)(2,1)} %get-tuple-element.24), calls=%async_computation | async-start | bytes 524288 | tf_op jit(solution)/shard_map/all_to_all | solution.py:42
  10.9 0.0 collective-permute-done.got_ref
  10.9 0.0 copy-start
  10.9 1.6 %collective-permute-start.2 = (bf16[64,128]{1,0:T(8,128)(2,1)S(1)}, bf16[64,128]{1,0:T(8,128)(2,1)S(1)}, u32[]{:S(2)}, u32[]{:S(2)}) collective-permute-start(bf16[64,128]{1,0:T(8,128)(2,1)S(1)} %get-tuple-element.32), channel_id=1, source_target_pairs={{0,16},{1,17},{2,18},{3,19},{4,20},{5,21},{6,22},{7,23},{8,24},{9,... | collective-permute-start | bytes 49160 | tf_op jit(solution)/shard_map/ppermute | solution.py:321
  12.4 1.4 %collective-permute-start.3 = (bf16[64,128]{1,0:T(8,128)(2,1)S(1)}, bf16[64,128]{1,0:T(8,128)(2,1)S(1)}, u32[]{:S(2)}, u32[]{:S(2)}) collective-permute-start(bf16[64,128]{1,0:T(8,128)(2,1)S(1)} %get-tuple-element.31), channel_id=1, source_target_pairs={{0,17},{1,16},{2,19},{3,18},{4,21},{5,20},{6,23},{7,22},{8,25},{9,... | collective-permute-start | bytes 49160 | tf_op jit(solution)/shard_map/ppermute | solution.py:321
  13.9 0.6 %collective-permute-start.1 = (bf16[64,128]{1,0:T(8,128)(2,1)S(1)}, bf16[64,128]{1,0:T(8,128)(2,1)S(1)}, u32[]{:S(2)}, u32[]{:S(2)}) collective-permute-start(bf16[64,128]{1,0:T(8,128)(2,1)S(1)} %get-tuple-element.31), channel_id=1, source_target_pairs={{0,1},{1,0},{2,3},{3,2},{4,5},{5,4},{6,7},{7,6},{8,9},{9,8},{10,11... | collective-permute-start | bytes 49160 | tf_op jit(solution)/shard_map/ppermute | solution.py:321
  14.4 1.7 %levels.1 = (f32[2,256,128]{2,1,0:T(8,128)S(1)}, bf16[2,256,128]{2,1,0:T(8,128)(2,1)S(1)}) custom-call(bf16[1024,128]{1,0:T(8,128)(2,1)S(1)} %get-tuple-element.28.low_ref, bf16[2,1024,256]{2,1,0:T(8,128)(2,1)} %basis_hbm.1), custom_call_target="tpu_custom_call" | custom-call | flops 134217728 | bytes 524288 | tf_op jit(solution)/shard_map/levels/pallas_call | solution.py:62
  16.2 0.0 collective-permute-done.2.refs_1_
  16.2 1.0 %collective-permute-done.3.refs_2_ = bf16[64,128]{1,0:T(8,128)(2,1)S(1)} collective-permute-done((bf16[64,128]{1,0:T(8,128)(2,1)S(1)}, bf16[64,128]{1,0:T(8,128)(2,1)S(1)}, u32[]{:S(2)}, u32[]{:S(2)}) %collective-permute-start.3) | collective-permute-done | bytes 16416 | tf_op jit(solution)/shard_map/ppermute | solution.py:321
  17.1 0.5 %collective-permute-done.1.refs_0_ = bf16[64,128]{1,0:T(8,128)(2,1)S(1)} collective-permute-done((bf16[64,128]{1,0:T(8,128)(2,1)S(1)}, bf16[64,128]{1,0:T(8,128)(2,1)S(1)}, u32[]{:S(2)}, u32[]{:S(2)}) %collective-permute-start.1) | collective-permute-done | bytes 16416 | tf_op jit(solution)/shard_map/ppermute | solution.py:321
  17.6 0.0 all-to-all-done.arrived_ref
  17.6 0.0 copy-done
  17.6 1.4 %middle.1 = (bf16[8,192,128]{2,1,0:T(8,128)(2,1)}, bf16[1024,128]{1,0:T(8,128)(2,1)S(1)}, f32[2,256,128]{2,1,0:T(8,128)S(1)}) custom-call(bf16[1024,1024]{1,0:T(8,128)(2,1)S(1)} %copy-done, bf16[8,128,128]{2,1,0:T(8,128)(2,1)S(1)} %all-to-all-done.arrived_ref, ...), custom_call_target="tpu_custom_call", output_to_operand_aliasing={{1}: (2, {}), {2}: (3, {})} | custom-call | flops 268435456 | bytes 1048576 | tf_op jit(solution)/shard_map/middle/pallas_call | solution.py:62
  19.0 5.5 %all-to-all-start.1 = ((bf16[8,192,128]{2,1,0:T(8,128)(2,1)}), bf16[8,192,128]{2,1,0:T(8,128)(2,1)S(1)}, u32[]{:S(2)}, u32[]{:S(2)}) async-start(bf16[8,192,128]{2,1,0:T(8,128)(2,1)} %get-tuple-element.33), calls=%async_computation.1 | async-start | bytes 786432 | tf_op jit(solution)/shard_map/all_to_all | solution.py:42
  24.5 0.0 collective-permute-start.4
  24.5 1.3 %collective-permute-done.4.got_ref.refs_0_ = bf16[2,256,128]{2,1,0:T(8,128)(2,1)S(1)} collective-permute-done((bf16[2,256,128]{2,1,0:T(8,128)(2,1)S(1)}, bf16[2,256,128]{2,1,0:T(8,128)(2,1)S(1)}, u32[]{:S(2)}, u32[]{:S(2)}) %collective-permute-start.4) | collective-permute-done | bytes 131104 | tf_op jit(solution)/shard_map/ppermute | solution.py:21
  25.9 1.6 %collective-permute-start.5 = (bf16[1,256,128]{2,1,0:T(8,128)(2,1)S(1)}, bf16[1,256,128]{2,1,0:T(8,128)(2,1)S(1)}, u32[]{:S(2)}, u32[]{:S(2)}) collective-permute-start(bf16[1,256,128]{2,1,0:T(8,128)(2,1)S(1)} %level_sum.1), channel_id=1, source_target_pairs={{0,16},{8,24},{16,0},{24,8},{1,17},{9,25},{17,1},{25,9},{2,18},{10... | collective-permute-start | bytes 196616 | tf_op jit(solution)/shard_map/ppermute | solution.py:21
  27.5 2.9 %dense.1 = (f32[1024,128]{1,0:T(8,128)S(1)}, bf16[2,1024,256]{2,1,0:T(8,128)(2,1)S(1)}, bf16[1024,1024]{1,0:T(8,128)(2,1)S(1)}, bf16[1024,256]{1,0:T(8,128)(2,1)S(1)}) custom-call(s32[8]{0:T(128)} %owner_hbm.3, bf16[1024,128]{1,0:T(8,128)(2,1)S(1)} %get-tuple-element.34.low_ref, bf16[1024,1024]{1,0:T(8,128)(2,1)} %inverse_hbm.1, ...), custom_call_target="tpu_custom_call" | custom-call | flops 268435456 | bytes 1048576 | tf_op jit(solution)/shard_map/dense/pallas_call | solution.py:62
  30.4 0.0 collective-permute-done.5.refs_1_
  30.4 0.4 %couple.1.partial_ref = f32[1024,128]{1,0:T(8,128)S(1)} custom-call(f32[1024,128]{1,0:T(8,128)S(1)} %get-tuple-element.35.dense_ref, bf16[2,1024,256]{2,1,0:T(8,128)(2,1)S(1)} %get-tuple-element.36.expand_ref, bf16[2,256,128]{2,1,0:T(8,128)(2,1)S(1)} %collective-permute-done.4.got_ref.refs_0_, bf16[1,256,128]{2,1,0:T(8,128)(2,1)S(1)} %collective-permute-done.5.refs_1_), custom_call_target="tpu_custom_call" | custom-call | flops 134217728 | bytes 524288 | tf_op jit(solution)/shard_map/couple/pallas_call | solution.py:62
  30.8 0.6 %all-to-all-done.1.returned_ref = bf16[8,192,128]{2,1,0:T(8,128)(2,1)S(1)} async-done(((bf16[8,192,128]{2,1,0:T(8,128)(2,1)}), bf16[8,192,128]{2,1,0:T(8,128)(2,1)S(1)}, u32[]{:S(2)}, u32[]{:S(2)}) %all-to-all-start.1) | async-done | bytes 393248 | tf_op jit(solution)/shard_map/all_to_all | solution.py:42
  31.5 0.1 collective-permute-start.6
  31.5 0.8 %expand.1.partial_ref = f32[1024,128]{1,0:T(8,128)S(1)} custom-call(f32[1024,128]{1,0:T(8,128)S(1)} %get-tuple-element.39.partial_ref, bf16[1024,1024]{1,0:T(8,128)(2,1)S(1)} %get-tuple-element.40.expand_ref, bf16[8,192,128]{2,1,0:T(8,128)(2,1)S(1)} %all-to-all-done.1.returned_ref, bf16[1024,256]{1,0:T(8,128)(2,1)S(1)} %get-tuple-element.41.root_expand_ref, ...), custom_call_target="tpu_custom_call" | custom-call | flops 268435456 | bytes 1048576 | tf_op jit(solution)/shard_map/expand/pallas_call | solution.py:62
  32.3 0.4 %collective-permute-done.6.other_ref = bf16[128,128]{1,0:T(8,128)(2,1)S(1)} collective-permute-done((bf16[128,128]{1,0:T(8,128)(2,1)S(1)}, bf16[128,128]{1,0:T(8,128)(2,1)S(1)}, u32[]{:S(2)}, u32[]{:S(2)}) %collective-permute-start.6) | collective-permute-done | bytes 32800 | tf_op jit(solution)/shard_map/ppermute | solution.py:21
  32.7 1.0 %final.1 = f32[1024,128]{1,0:T(8,128)} custom-call(f32[1024,128]{1,0:T(8,128)S(1)} %expand.1.partial_ref, bf16[1024,256]{1,0:T(8,128)(2,1)S(1)} %get-tuple-element.41.root_expand_ref, bf16[128,128]{1,0:T(8,128)(2,1)S(1)} %collective-permute-done.6.other_ref), custom_call_target="tpu_custom_call" | custom-call | flops 67108864 | bytes 262144 | tf_op jit(solution)/shard_map/final/pallas_call | solution.py:62
  (3 shorter events, 0.1 us)
Async XLA Ops:
  2.9 7.9 %collective-permute-start = (f32[128,128]{1,0:T(8,128)S(1)}, f32[128,128]{1,0:T(8,128)S(1)}, u32[]{:S(2)}, u32[]{:S(2)}) collective-permute-start(f32[128,128]{1,0:T(8,128)S(1)} %get-tuple-element.26), channel_id=1, source_target_pairs={{0,8},{8,0},{16,24},{24,16},{1,9},{9,1},{17,25},{25,17},{2,10},{10... | collective-permute-start | bytes 196616 | tf_op jit(solution)/shard_map/ppermute | solution.py:21
  3.4 14.2 %all-to-all-start = ((bf16[8,128,128]{2,1,0:T(8,128)(2,1)}), bf16[8,128,128]{2,1,0:T(8,128)(2,1)S(1)}, u32[]{:S(2)}, u32[]{:S(2)}) async-start(bf16[8,128,128]{2,1,0:T(8,128)(2,1)} %get-tuple-element.24), calls=%async_computation | async-start | bytes 524288 | tf_op jit(solution)/shard_map/all_to_all | solution.py:42
  10.9 6.8 %copy-start = (bf16[1024,1024]{1,0:T(8,128)(2,1)S(1)}, bf16[1024,1024]{1,0:T(8,128)(2,1)}, u32[]{:S(2)}) copy-start(bf16[1024,1024]{1,0:T(8,128)(2,1)} %middle_ref.1) | copy-start | bytes 6291460
  10.9 5.3 %collective-permute-start.2 = (bf16[64,128]{1,0:T(8,128)(2,1)S(1)}, bf16[64,128]{1,0:T(8,128)(2,1)S(1)}, u32[]{:S(2)}, u32[]{:S(2)}) collective-permute-start(bf16[64,128]{1,0:T(8,128)(2,1)S(1)} %get-tuple-element.32), channel_id=1, source_target_pairs={{0,16},{1,17},{2,18},{3,19},{4,20},{5,21},{6,22},{7,23},{8,24},{9,... | collective-permute-start | bytes 49160 | tf_op jit(solution)/shard_map/ppermute | solution.py:321
  12.4 4.7 %collective-permute-start.3 = (bf16[64,128]{1,0:T(8,128)(2,1)S(1)}, bf16[64,128]{1,0:T(8,128)(2,1)S(1)}, u32[]{:S(2)}, u32[]{:S(2)}) collective-permute-start(bf16[64,128]{1,0:T(8,128)(2,1)S(1)} %get-tuple-element.31), channel_id=1, source_target_pairs={{0,17},{1,16},{2,19},{3,18},{4,21},{5,20},{6,23},{7,22},{8,25},{9,... | collective-permute-start | bytes 49160 | tf_op jit(solution)/shard_map/ppermute | solution.py:321
  13.9 3.7 %collective-permute-start.1 = (bf16[64,128]{1,0:T(8,128)(2,1)S(1)}, bf16[64,128]{1,0:T(8,128)(2,1)S(1)}, u32[]{:S(2)}, u32[]{:S(2)}) collective-permute-start(bf16[64,128]{1,0:T(8,128)(2,1)S(1)} %get-tuple-element.31), channel_id=1, source_target_pairs={{0,1},{1,0},{2,3},{3,2},{4,5},{5,4},{6,7},{7,6},{8,9},{9,8},{10,11... | collective-permute-start | bytes 49160 | tf_op jit(solution)/shard_map/ppermute | solution.py:321
  19.0 12.4 %all-to-all-start.1 = ((bf16[8,192,128]{2,1,0:T(8,128)(2,1)}), bf16[8,192,128]{2,1,0:T(8,128)(2,1)S(1)}, u32[]{:S(2)}, u32[]{:S(2)}) async-start(bf16[8,192,128]{2,1,0:T(8,128)(2,1)} %get-tuple-element.33), calls=%async_computation.1 | async-start | bytes 786432 | tf_op jit(solution)/shard_map/all_to_all | solution.py:42
  24.5 1.3 %collective-permute-start.4 = (bf16[2,256,128]{2,1,0:T(8,128)(2,1)S(1)}, bf16[2,256,128]{2,1,0:T(8,128)(2,1)S(1)}, u32[]{:S(2)}, u32[]{:S(2)}) collective-permute-start(bf16[2,256,128]{2,1,0:T(8,128)(2,1)S(1)} %get-tuple-element.37), channel_id=1, source_target_pairs={{0,8},{8,0},{16,24},{24,16},{1,9},{9,1},{17,25},{25,17},{2,10},{10... | collective-permute-start | bytes 393224 | tf_op jit(solution)/shard_map/ppermute | solution.py:21
  25.9 4.5 %collective-permute-start.5 = (bf16[1,256,128]{2,1,0:T(8,128)(2,1)S(1)}, bf16[1,256,128]{2,1,0:T(8,128)(2,1)S(1)}, u32[]{:S(2)}, u32[]{:S(2)}) collective-permute-start(bf16[1,256,128]{2,1,0:T(8,128)(2,1)S(1)} %level_sum.1), channel_id=1, source_target_pairs={{0,16},{8,24},{16,0},{24,8},{1,17},{9,25},{17,1},{25,9},{2,18},{10... | collective-permute-start | bytes 196616 | tf_op jit(solution)/shard_map/ppermute | solution.py:21
  31.5 1.3 %collective-permute-start.6 = (bf16[128,128]{1,0:T(8,128)(2,1)S(1)}, bf16[128,128]{1,0:T(8,128)(2,1)S(1)}, u32[]{:S(2)}, u32[]{:S(2)}) collective-permute-start(bf16[128,128]{1,0:T(8,128)(2,1)S(1)} %get-tuple-element.42.mine_ref), channel_id=1, source_target_pairs={{0,8},{8,0},{16,24},{24,16},{1,9},{9,1},{17,25},{25,17},{2,10},{10... | collective-permute-start | bytes 98312 | tf_op jit(solution)/shard_map/ppermute | solution.py:21
